TPU v7x, 32 devices: a whole 2x2x4 slice. The times are simulated.
32 devices in a mesh: groups: 1, tile: 16 (over z, y, x), col: 2 (over core).
Axes of the slice: x: 2, y: 2, z: 4, core: 2. Of those that a mesh axis runs over, the one named last changes fastest.
Arguments:
- zonal_velocity: float32 [50, 512, 256], P(None, ('groups', 'tile'), 'col'), may hold values from -4 to 4
- meridional_velocity: float32 [50, 512, 256], P(None, ('groups', 'tile'), 'col'), may hold values from -4 to 4
- surface_height: float32 [512, 256], P(('groups', 'tile'), 'col'), may hold values from -3 to 3
- thickness: float32 [50], replicated, may hold values from 0.5 to 2
- mixing: float32 [50], replicated, may hold values from 0.02 to 0.2
- ocean_wet: int32 [512, 256], P(('groups', 'tile'), 'col'), may hold values from 0 to 1, as said below
- spectra: float32 [36, 32, 128, 256], P(None, None, ('groups', 'tile'), 'col'), may hold values from 0.1 to 3
- wind_speed: float32 [128, 256], P(('groups', 'tile'), 'col'), may hold values from 1 to 10
- wind_direction: float32 [128, 256], P(('groups', 'tile'), 'col'), may hold values from -3.140625 to 3.140625
- wave_wet: int32 [128, 256], P(('groups', 'tile'), 'col'), may hold values from 0 to 1, as said below
- remap_source: int32 [32, 8, 512], P(('groups', 'tile', 'col')), may hold values from 0 to 4096, as said below
- remap_target: int32 [32, 8, 512], P(('groups', 'tile', 'col')), may hold values from 0 to 1024, as said below
- remap_weight: float32 [32, 8, 512], P(('groups', 'tile', 'col')), as said below
Outputs:
- new_zonal: float32 [50, 512, 256], P(None, ('groups', 'tile'), 'col')
- new_meridional: float32 [50, 512, 256], P(None, ('groups', 'tile'), 'col')
- new_height: float32 [512, 256], P(('groups', 'tile'), 'col')
- new_spectra: float32 [36, 32, 128, 256], P(None, None, ('groups', 'tile'), 'col')
Inputs may be any that keep to these rules, and one draw needn't show every extreme that they name: `ocean_wet`: 1 marks sea. `wave_wet`: 1 exactly where the 2x2 block of ocean cells under the wave cell (ocean rows 2y, 2y+1, columns 2x, 2x+1) holds sea. `remap_source`: block [s, j] lists, in row-major order and from slot 0 on, the sea cells of rank s in its local columns j * 2 * 8 to (j + 1) * 2 * 8 - 1, as local index row * 128 + column; the remaining slots hold 4096. Every sea cell appears in exactly one entry. In every draw some rank holds the wave cells of 8 full blocks, one from each rank that sends to it. `remap_target`: for each live entry the wave cell on rank d that the entry links to, as local index column * 128 + row, in the slot of the entry in its source block; padded entries hold 1024. `remap_weight`: positive on live entries, summing to 1 over the entries that end in one wave cell; 0 on padded entries.
All inputs are finite; a program needn't handle non-finite values.
Results may differ from a plain program's by a relative error of at most 0.00015.
Values sent between devices are 32-bit elements; how exact they have to be, the bound alone decides.
A program may use at most 192 MiB of HBM per device.

v0:
```python
import math

import jax
import jax.numpy as jnp
from jax import lax
from jax.sharding import PartitionSpec as P

ND = 36
NF = 32
WSTEPS = 4
OSTEPS = 4


def padded_2(value, sides, width):
    for axis, dim in sides:
        count, length = (lax.axis_size(axis), value.shape[dim])
        up = [(i, (i + 1) % count) for i in range(count - 1)]
        down = [(j, i) for i, j in up]
        last = lax.slice_in_dim(value, length - width, length, axis=dim)
        initial = lax.slice_in_dim(value, 0, width, axis=dim)
        before = lax.ppermute(last, axis, up)
        after = lax.ppermute(initial, axis, down)
        value = jnp.concatenate([before, value, after], axis=dim)
    return value


def spectral_tables():
    angles = (jnp.arange(ND, dtype=jnp.float32) + 0.5) * (2.0 * math.pi / ND)
    group_speed = 0.5 * jnp.power(jnp.float32(1.1), -jnp.arange(NF, dtype=jnp.float32))
    freq_weight = 2.0 * (jnp.arange(NF, dtype=jnp.float32) + 1.0) / NF
    return (jnp.cos(angles), jnp.sin(angles), group_speed, freq_weight)


def source_term(energy, fields, tables):
    cos_dir, sin_dir, group_speed, freq_weight = tables
    downwind = jnp.maximum(
        fields[3][None] * cos_dir[:, None, None] + fields[4][None] * sin_dir[:, None, None], 0.0
    )
    column_mean = jnp.mean(energy, axis=(0, 1))
    damping = 0.3 * jnp.exp(-0.5 * fields[5]) * column_mean
    growth = 0.02 * downwind[:, None] * freq_weight[None, :, None, None] - damping[None, None]
    return energy * jnp.exp(growth)


def advect(padded, fields, tables):
    cos_dir, sin_dir, group_speed, freq_weight = tables
    drift_x, drift_y, wet_cells = (fields[0], fields[1], fields[2])
    speed_grid = group_speed[None, :, None, None]
    velocity_x = speed_grid * cos_dir[:, None, None, None] + drift_x[None, None]
    velocity_y = speed_grid * sin_dir[:, None, None, None] + drift_y[None, None]
    face_x = 0.5 * (velocity_x[:, :, :-1, 1:-1] + velocity_x[:, :, 1:, 1:-1])
    open_x = wet_cells[:-1, 1:-1] * wet_cells[1:, 1:-1]
    flux_x = (
        jnp.maximum(face_x, 0.0) * padded[:, :, :-1, 1:-1]
        + jnp.minimum(face_x, 0.0) * padded[:, :, 1:, 1:-1]
    ) * open_x
    face_y = 0.5 * (velocity_y[:, :, 1:-1, :-1] + velocity_y[:, :, 1:-1, 1:])
    open_y = wet_cells[1:-1, :-1] * wet_cells[1:-1, 1:]
    flux_y = (
        jnp.maximum(face_y, 0.0) * padded[:, :, 1:-1, :-1]
        + jnp.minimum(face_y, 0.0) * padded[:, :, 1:-1, 1:]
    ) * open_y
    return (
        padded[:, :, 1:-1, 1:-1]
        - (flux_x[:, :, 1:] - flux_x[:, :, :-1])
        - (flux_y[:, :, :, 1:] - flux_y[:, :, :, :-1])
    )


def radiation_stress(energy, tables):
    cos_dir, sin_dir = (tables[0], tables[1])
    moments = jnp.stack([cos_dir * cos_dir, cos_dir * sin_dir, sin_dir * sin_dir]) * (
        0.5 / (ND * NF)
    )
    per_direction = jnp.sum(energy, axis=1)
    return jnp.einsum("cd,dxy->cxy", moments, per_direction, precision=lax.Precision.HIGHEST)


def mixing_tendency(profile, top_force, mixing, thickness):
    interface_flux = mixing[1:, None, None] * (profile[:-1] - profile[1:])
    bottom = mixing[0] * profile[-1:]
    fluxes = jnp.concatenate([top_force[None], interface_flux, bottom], axis=0)
    return (fluxes[:-1] - fluxes[1:]) / thickness[:, None, None]


def centered(extended):
    slope_x = 0.5 * (extended[..., 1:-1, 2:] - extended[..., 1:-1, :-2])
    slope_y = 0.5 * (extended[..., 2:, 1:-1] - extended[..., :-2, 1:-1])
    return (slope_x, slope_y)


def route_blocks(blocks, toward_waves):
    tile_count = lax.axis_size("tile")
    col_count = lax.axis_size("col")
    peer_count = blocks.shape[1]
    slot_count = blocks.shape[2]
    tile_index = lax.axis_index("tile")
    col_index = lax.axis_index("col")
    anchor = jnp.zeros((), jnp.int32)
    spread = jnp.zeros((3, tile_count, slot_count), jnp.float32)
    spread = lax.dynamic_update_slice(spread, blocks, (anchor, col_index * peer_count, anchor))
    flattened = spread.reshape(3, tile_count * slot_count)
    if toward_waves:
        delivered = lax.all_to_all(
            lax.all_to_all(flattened, "tile", split_axis=1, concat_axis=1, tiled=True),
            "col",
            split_axis=1,
            concat_axis=1,
            tiled=True,
        )
    else:
        delivered = lax.all_to_all(
            lax.all_to_all(flattened, "tile", split_axis=1, concat_axis=1, tiled=True),
            "col",
            split_axis=1,
            concat_axis=1,
            tiled=True,
        )
    delivered = delivered.reshape(3, col_count, peer_count, slot_count)
    return lax.dynamic_index_in_dim(delivered, tile_index // peer_count, 1, keepdims=False)


def body(
    zonal_velocity,
    meridional_velocity,
    surface_height,
    thickness,
    mixing,
    ocean_wet,
    spectra,
    wind_speed,
    wind_direction,
    wave_wet,
    remap_source,
    remap_target,
    remap_weight,
):
    tables = spectral_tables()
    tile_count = lax.axis_size("tile")
    col_count = lax.axis_size("col")
    tile_rows, tile_cols = surface_height.shape
    span_x, span_y = wave_wet.shape
    peer_count = remap_source.shape[1]
    slot_count = remap_source.shape[2]
    sea_cells = ocean_wet.astype(jnp.float32)
    wet_cells = wave_wet.astype(jnp.float32)
    zonal_flow = zonal_velocity * sea_cells[None]
    meridional = meridional_velocity * sea_cells[None]
    height = surface_height
    energy = spectra * wet_cells[None, None]
    sources = remap_source[0].reshape(peer_count * slot_count)
    targets = remap_target[0].reshape(peer_count * slot_count)
    weights = remap_weight[0]
    surface = jnp.stack([zonal_flow[0], meridional[0], height]).reshape(3, tile_rows * tile_cols)
    surface = jnp.concatenate([surface, jnp.zeros((3, 1), jnp.float32)], axis=1)
    outgoing = jnp.take(surface, sources, axis=1).reshape(3, peer_count, slot_count) * weights[None]
    arrived = route_blocks(outgoing, True)
    currents = (
        jnp.zeros((3, span_x * span_y + 1), jnp.float32)
        .at[:, targets]
        .add(arrived.reshape(3, peer_count * slot_count))
    )
    currents = currents[:, :-1].reshape(3, span_x, span_y)
    stress = radiation_stress(energy, tables).reshape(3, span_x * span_y)
    stress = jnp.concatenate([stress, jnp.zeros((3, 1), jnp.float32)], axis=1)
    returning = jnp.take(stress, targets, axis=1).reshape(3, peer_count, slot_count)
    returned = route_blocks(returning, False)
    ocean_stress = (
        jnp.zeros((3, tile_rows * tile_cols + 1), jnp.float32)
        .at[:, sources]
        .add(returned.reshape(3, peer_count * slot_count))
    )
    ocean_stress = ocean_stress[:, :-1].reshape(3, tile_rows, tile_cols)
    fields = jnp.stack(
        [
            0.03 * currents[0],
            0.03 * currents[1],
            wet_cells,
            wind_speed * jnp.cos(wind_direction),
            wind_speed * jnp.sin(wind_direction),
            currents[2],
        ]
    )
    wide_fields = padded_2(fields, (("tile", 1), ("col", 2)), 2)
    inner_fields = wide_fields[:, 1:-1, 1:-1]
    for section_index in range(WSTEPS):
        energy = source_term(energy, fields, tables)
        padded = padded_2(energy, (("tile", 2), ("col", 3)), 1)
        energy = advect(padded, inner_fields, tables)
    row_start = lax.axis_index("tile") * tile_rows
    col_start = lax.axis_index("col") * tile_cols
    total_rows = tile_rows * tile_count
    total_cols = tile_cols * col_count
    coriolis = (
        0.1 + 0.1 * ((row_start + jnp.arange(tile_rows)).astype(jnp.float32) + 0.5) / total_rows
    )[:, None]
    edge_rows = row_start + jnp.arange(-1, tile_rows + 1)
    edge_cols = col_start + jnp.arange(-1, tile_cols + 1)
    inside = (
        ((edge_rows >= 0) & (edge_rows < total_rows))[:, None]
        & ((edge_cols >= 0) & (edge_cols < total_cols))[None, :]
    ).astype(jnp.float32)
    column_depth = jnp.sum(thickness)
    force_x = jnp.zeros_like(height)
    force_y = jnp.zeros_like(height)
    for iteration in range(OSTEPS):
        transport_x = jnp.sum(thickness[:, None, None] * zonal_flow, axis=0) / column_depth
        transport_y = jnp.sum(thickness[:, None, None] * meridional, axis=0) / column_depth
        carried = jnp.stack([transport_x, transport_y, height])
        if iteration == 0:
            carried = jnp.concatenate([carried, ocean_stress], axis=0)
        border = padded_2(carried, (("tile", 1), ("col", 2)), 2)
        if iteration == 0:
            slope_x, slope_y = centered(border[3:, 1:-1, 1:-1])
            force_x = -0.5 * (slope_x[0] + slope_y[1])
            force_y = -0.5 * (slope_x[1] + slope_y[2])
        diverge_x = 0.5 * (border[0, 1:-1, 2:] - border[0, 1:-1, :-2])
        diverge_y = 0.5 * (border[1, 2:, 1:-1] - border[1, :-2, 1:-1])
        margin_height = (border[2, 1:-1, 1:-1] - 0.2 * (diverge_x + diverge_y)) * inside
        slope_x, slope_y = centered(margin_height)
        pressure_x = 0.2 * slope_x
        pressure_y = 0.2 * slope_y
        new_zonal = (
            zonal_flow
            + coriolis * meridional
            - pressure_x
            + mixing_tendency(zonal_flow, force_x, mixing, thickness)
        ) * sea_cells[None]
        new_meridional = (
            meridional
            - coriolis * zonal_flow
            - pressure_y
            + mixing_tendency(meridional, force_y, mixing, thickness)
        ) * sea_cells[None]
        zonal_flow, meridional = (new_zonal, new_meridional)
        height = margin_height[1:-1, 1:-1]
    return (zonal_flow, meridional, height, energy)


def solution(mesh):
    return jax.shard_map(
        body,
        mesh=mesh,
        in_specs=(
            P(None, ("groups", "tile"), "col"),
            P(None, ("groups", "tile"), "col"),
            P(("groups", "tile"), "col"),
            P(),
            P(),
            P(("groups", "tile"), "col"),
            P(None, None, ("groups", "tile"), "col"),
            P(("groups", "tile"), "col"),
            P(("groups", "tile"), "col"),
            P(("groups", "tile"), "col"),
            P(("groups", "tile", "col"), None, None),
            P(("groups", "tile", "col"), None, None),
            P(("groups", "tile", "col"), None, None),
        ),
        out_specs=(
            P(None, ("groups", "tile"), "col"),
            P(None, ("groups", "tile"), "col"),
            P(("groups", "tile"), "col"),
            P(None, None, ("groups", "tile"), "col"),
        ),
        check_vma=False,
    )
```

profile of v0, /device:TPU:18, one launch (start us, length us, event | category | flops | bytes accessed | tf_op | source)
XLA Modules:
  0.0 606.1 jit_solution(10619740201724366710)
XLA Ops:
  8.7 10.8 %gather_fusion = f32[4096,3]{1,0:T(8,128)S(1)} fusion(f32[3,1025]{0,1:T(8,128)S(1)} %concatenate.192.clone, s32[4096]{0:T(1024)S(1)} %get-tuple-element.124), kind=kCustom, calls=%fused_computation | custom fusion | bytes 114688 | tf_op jit(solution)/shard_map/jit(_take)/gather | solution.py:166
  21.4 7.1 %all-to-all-start = ((f32[3,16,512]{2,0,1:T(4,128)}), f32[3,16,512]{2,0,1:T(4,128)S(1)}, u32[]{:S(2)}, u32[]{:S(2)}) async-start(f32[3,16,512]{2,0,1:T(4,128)} %select_dynamic-update-slice_fusion), calls=%async_computation | async-start | bytes 262144 | tf_op jit(solution)/shard_map/all_to_all | solution.py:113
  40.2 15.8 %gather_fusion.1 = f32[4096,3]{1,0:T(8,128)} fusion(f32[3,4097]{0,1:T(8,128)} %concatenate.228, s32[4096]{0:T(1024)S(1)} %copy-done.51), kind=kCustom, calls=%fused_computation.1 | custom fusion | bytes 114688 | tf_op jit(solution)/shard_map/jit(_take)/gather | solution.py:156
  64.6 6.9 %all-to-all-start.2 = ((f32[3,16,512]{2,0,1:T(4,128)}), f32[3,16,512]{2,0,1:T(4,128)S(1)}, u32[]{:S(2)}, u32[]{:S(2)}) async-start(f32[3,16,512]{2,0,1:T(4,128)} %multiply_dynamic-update-slice_fusion), calls=%async_computation.2 | async-start | bytes 262144 | tf_op jit(solution)/shard_map/all_to_all | solution.py:105
  73.6 25.4 %scatter_custom_fusion = f32[3,4097]{0,1:T(8,128)} fusion(s32[4096]{0:T(1024)} %bitcast.149, f32[4096,3]{1,0:T(8,128)} %copy.78, f32[]{:T(128)} %constant.128.clone.1), kind=kCustom, calls=%fused_computation.109 | custom fusion | flops 12288 | bytes 49676 | tf_op jit(solution)/shard_map/scatter-add | solution.py:171
  116.8 24.5 %scatter_custom_fusion.1 = f32[3,1025]{0,1:T(8,128)S(1)} fusion(s32[4096]{0:T(1024)} %bitcast.147, f32[4096,3]{1,0:T(8,128)} %copy.83, f32[]{:T(128)} %constant.128.clone.1), kind=kCustom, calls=%fused_computation.175 | custom fusion | flops 12288 | bytes 12812 | tf_op jit(solution)/shard_map/scatter-add | solution.py:161
  162.6 15.3 %collective-permute-done.17 = f32[6,2,128]{2,1,0:T(2,128)S(1)} collective-permute-done((f32[6,2,128]{2,1,0:T(2,128)S(1)}, f32[6,2,128]{2,1,0:T(2,128)S(1)}, u32[]{:S(2)}, u32[]{:S(2)}) %collective-permute-start.17) | collective-permute-done | bytes 6176 | tf_op jit(solution)/shard_map/ppermute | solution.py:22
  242.3 6.6 %fusion.156 = (f32[36,32,10,1]{3,1,2,0:T(8,128)}, f32[36,32,10,1]{3,1,2,0:T(8,128)}) fusion(f32[36,32,10,128]{3,1,2,0:T(8,128)S(1)} %pad_maximum_fusion.24), kind=kLoop, calls=%fused_computation.386 | loop fusion | bytes 184320 | tf_op jit(solution)/shard_map/slice | solution.py:19
  264.2 15.6 %fusion.19 = (f32[36,32,9,128]{3,1,2,0:T(8,128)}, f32[36,32,9,128]{3,1,2,0:T(8,128)}) fusion(f32[36,32,8,128]{3,1,2,0:T(8,128)} %copy-done.3, f32[36,32,1,128]{3,1,2,0:T(8,128)S(1)} %collective-permute-done.20, f32[36,32,1,128]{3,1,2,0:T(8,128)S(1)} %collective-permute-done.21, f32[9,128]{1,0:T(8,128)S(1)} %copy-done.33, ...), kind=kLoop, calls=%fused_computation.60 | loop fusion | flops 13271040 | bytes 27136512 | tf_op jit(solution)/shard_map/mul | solution.py:53
  279.8 6.3 %copy.87 = f32[36,32,10,1]{3,1,2,0:T(8,128)} copy(f32[36,32,10,1]{0,1,3,2:T(8,128)S(1)} %collective-permute-done.23) | data formatting | bytes 92160 | tf_op jit(solution)/shard_map/ppermute | solution.py:22
  286.1 7.2 %copy.85 = f32[36,32,10,1]{3,1,2,0:T(8,128)} copy(f32[36,32,10,1]{0,1,3,2:T(8,128)} %collective-permute-done.22) | data formatting | bytes 92160 | tf_op jit(solution)/shard_map/ppermute | solution.py:21
  293.4 17.5 %fusion.14 = (f32[36,32,8,129]{3,1,2,0:T(8,128)S(1)}, f32[36,32,8,129]{3,1,2,0:T(8,128)}) fusion(f32[36,32,10,1]{3,1,2,0:T(8,128)} %copy.87, f32[36,32,1,128]{3,1,2,0:T(8,128)S(1)} %collective-permute-done.21, f32[36,32,8,128]{3,1,2,0:T(8,128)} %copy-done.3, f32[36,32,1,128]{3,1,2,0:T(8,128)S(1)} %collective-permute-done.20, f32[36,32,10,1]{3,1,2,0:T(8,128)} %copy.85, ...), kind=kLoop, calls=%fused_computation.41 | loop fusion | flops 16644096 | bytes 25016352 | tf_op jit(solution)/shard_map/mul | solution.py:59
  329.5 8.8 %collective-permute-done.25 = f32[36,32,1,128]{3,1,2,0:T(8,128)S(1)} collective-permute-done((f32[36,32,1,128]{3,1,2,0:T(8,128)S(1)}, f32[36,32,1,128]{3,1,2,0:T(8,128)S(1)}, u32[]{:S(2)}, u32[]{:S(2)}) %collective-permute-start.25) | collective-permute-done | bytes 589856 | tf_op jit(solution)/shard_map/ppermute | solution.py:22
  338.3 12.4 %collective-permute-done.24 = f32[36,32,1,128]{3,1,2,0:T(8,128)S(1)} collective-permute-done((f32[36,32,1,128]{3,1,2,0:T(8,128)S(1)}, f32[36,32,1,128]{3,1,2,0:T(8,128)S(1)}, u32[]{:S(2)}, u32[]{:S(2)}) %collective-permute-start.24) | collective-permute-done | bytes 589856 | tf_op jit(solution)/shard_map/ppermute | solution.py:21
  351.4 6.4 %fusion.155 = (f32[36,32,10,1]{3,1,2,0:T(8,128)}, f32[36,32,10,1]{3,1,2,0:T(8,128)}) fusion(f32[36,32,10,128]{3,1,2,0:T(8,128)S(1)} %pad_maximum_fusion.25), kind=kLoop, calls=%fused_computation.385 | loop fusion | bytes 184320 | tf_op jit(solution)/shard_map/slice | solution.py:19
  373.2 8.6 %fusion.21 = f32[36,32,9,128]{3,1,2,0:T(8,128)} fusion(f32[36,32,8,128]{3,1,2,0:T(8,128)} %copy-done.2, f32[36,32,1,128]{3,1,2,0:T(8,128)S(1)} %collective-permute-done.24, f32[36,32,1,128]{3,1,2,0:T(8,128)S(1)} %collective-permute-done.25, f32[36,32,9,128]{3,1,2,0:T(8,128)} %get-tuple-element.37, f32[9,128]{1,0:T(8,128)S(1)} %copy-done.34), kind=kLoop, calls=%fused_computation.64 | loop fusion | flops 10616832 | bytes 16519680 | tf_op jit(solution)/shard_map/mul | solution.py:53
  381.9 6.3 %copy.91 = f32[36,32,10,1]{3,1,2,0:T(8,128)} copy(f32[36,32,10,1]{0,1,3,2:T(8,128)S(1)} %collective-permute-done.27) | data formatting | bytes 92160 | tf_op jit(solution)/shard_map/ppermute | solution.py:22
  388.2 7.2 %copy.89 = f32[36,32,10,1]{3,1,2,0:T(8,128)} copy(f32[36,32,10,1]{0,1,3,2:T(8,128)} %collective-permute-done.26) | data formatting | bytes 92160 | tf_op jit(solution)/shard_map/ppermute | solution.py:21
  395.5 12.1 %fusion.10 = f32[36,32,8,129]{3,1,2,0:T(8,128)S(1)} fusion(f32[36,32,10,1]{3,1,2,0:T(8,128)} %copy.91, f32[36,32,1,128]{3,1,2,0:T(8,128)S(1)} %collective-permute-done.25, f32[36,32,8,128]{3,1,2,0:T(8,128)} %copy-done.2, f32[36,32,1,128]{3,1,2,0:T(8,128)S(1)} %collective-permute-done.24, f32[36,32,10,1]{3,1,2,0:T(8,128)} %copy.89, ...), kind=kLoop, calls=%fused_computation.31 | loop fusion | flops 14266368 | bytes 15505440 | tf_op jit(solution)/shard_map/mul | solution.py:59
  434.3 8.3 %collective-permute-done.28 = f32[36,32,1,128]{3,1,2,0:T(8,128)S(1)} collective-permute-done((f32[36,32,1,128]{3,1,2,0:T(8,128)S(1)}, f32[36,32,1,128]{3,1,2,0:T(8,128)S(1)}, u32[]{:S(2)}, u32[]{:S(2)}) %collective-permute-start.28) | collective-permute-done | bytes 589856 | tf_op jit(solution)/shard_map/ppermute | solution.py:21
  443.2 6.4 %fusion.154 = (f32[36,32,10,1]{3,1,2,0:T(8,128)}, f32[36,32,10,1]{3,1,2,0:T(8,128)}) fusion(f32[36,32,10,128]{3,1,2,0:T(8,128)S(1)} %pad_maximum_fusion.26), kind=kLoop, calls=%fused_computation.384 | loop fusion | bytes 184320 | tf_op jit(solution)/shard_map/slice | solution.py:19
  465.0 8.6 %fusion.23 = f32[36,32,9,128]{3,1,2,0:T(8,128)} fusion(f32[36,32,8,128]{3,1,2,0:T(8,128)} %copy-done, f32[36,32,1,128]{3,1,2,0:T(8,128)S(1)} %collective-permute-done.28, f32[36,32,1,128]{3,1,2,0:T(8,128)S(1)} %collective-permute-done.29, f32[36,32,9,128]{3,1,2,0:T(8,128)} %get-tuple-element.37, f32[9,128]{1,0:T(8,128)S(1)} %copy-done.35), kind=kLoop, calls=%fused_computation.68 | loop fusion | flops 10616832 | bytes 16519680 | tf_op jit(solution)/shard_map/mul | solution.py:53
  473.6 6.3 %copy.95 = f32[36,32,10,1]{3,1,2,0:T(8,128)} copy(f32[36,32,10,1]{0,1,3,2:T(8,128)S(1)} %collective-permute-done.31) | data formatting | bytes 92160 | tf_op jit(solution)/shard_map/ppermute | solution.py:22
  480.0 7.2 %copy.93 = f32[36,32,10,1]{3,1,2,0:T(8,128)} copy(f32[36,32,10,1]{0,1,3,2:T(8,128)} %collective-permute-done.30) | data formatting | bytes 92160 | tf_op jit(solution)/shard_map/ppermute | solution.py:21
  487.2 12.1 %fusion.6 = f32[36,32,8,129]{3,1,2,0:T(8,128)S(1)} fusion(f32[36,32,10,1]{3,1,2,0:T(8,128)} %copy.95, f32[36,32,1,128]{3,1,2,0:T(8,128)S(1)} %collective-permute-done.29, f32[36,32,8,128]{3,1,2,0:T(8,128)} %copy-done, f32[36,32,1,128]{3,1,2,0:T(8,128)S(1)} %collective-permute-done.28, f32[36,32,10,1]{3,1,2,0:T(8,128)} %copy.93, ...), kind=kLoop, calls=%fused_computation.21 | loop fusion | flops 14266368 | bytes 15505440 | tf_op jit(solution)/shard_map/mul | solution.py:59
  516.5 9.7 %collective-permute-done.33 = f32[36,32,1,128]{3,1,2,0:T(8,128)S(1)} collective-permute-done((f32[36,32,1,128]{3,1,2,0:T(8,128)S(1)}, f32[36,32,1,128]{3,1,2,0:T(8,128)S(1)}, u32[]{:S(2)}, u32[]{:S(2)}) %collective-permute-start.33) | collective-permute-done | bytes 589856 | tf_op jit(solution)/shard_map/ppermute | solution.py:22
  526.2 12.4 %collective-permute-done.32 = f32[36,32,1,128]{3,1,2,0:T(8,128)S(1)} collective-permute-done((f32[36,32,1,128]{3,1,2,0:T(8,128)S(1)}, f32[36,32,1,128]{3,1,2,0:T(8,128)S(1)}, u32[]{:S(2)}, u32[]{:S(2)}) %collective-permute-start.32) | collective-permute-done | bytes 589856 | tf_op jit(solution)/shard_map/ppermute | solution.py:21
  539.3 6.4 %fusion.153 = (f32[36,32,10,1]{3,1,2,0:T(8,128)}, f32[36,32,10,1]{3,1,2,0:T(8,128)}) fusion(f32[36,32,10,128]{3,1,2,0:T(8,128)S(1)} %pad_maximum_fusion.27), kind=kLoop, calls=%fused_computation.383 | loop fusion | bytes 184320 | tf_op jit(solution)/shard_map/slice | solution.py:19
  560.4 8.6 %fusion.25 = f32[36,32,9,128]{3,1,2,0:T(8,128)} fusion(f32[36,32,8,128]{3,1,2,0:T(8,128)} %copy-done.1, f32[36,32,1,128]{3,1,2,0:T(8,128)S(1)} %collective-permute-done.32, f32[36,32,1,128]{3,1,2,0:T(8,128)S(1)} %collective-permute-done.33, f32[36,32,9,128]{3,1,2,0:T(8,128)} %get-tuple-element.37, f32[9,128]{1,0:T(8,128)S(1)} %copy-done.35), kind=kLoop, calls=%fused_computation.72 | loop fusion | flops 10616832 | bytes 16519680 | tf_op jit(solution)/shard_map/mul | solution.py:53
  575.4 6.3 %copy.97 = f32[36,32,10,1]{3,1,2,0:T(8,128)} copy(f32[36,32,10,1]{0,1,3,2:T(8,128)S(1)} %collective-permute-done.34) | data formatting | bytes 92160 | tf_op jit(solution)/shard_map/ppermute | solution.py:21
  581.7 12.0 %fusion.2 = f32[36,32,8,129]{3,1,2,0:T(8,128)S(1)} fusion(f32[36,32,10,1]{3,1,2,0:T(8,128)} %copy.99, f32[36,32,1,128]{3,1,2,0:T(8,128)S(1)} %collective-permute-done.33, f32[36,32,8,128]{3,1,2,0:T(8,128)} %copy-done.1, f32[36,32,1,128]{3,1,2,0:T(8,128)S(1)} %collective-permute-done.32, f32[36,32,10,1]{3,1,2,0:T(8,128)} %copy.97, ...), kind=kLoop, calls=%fused_computation.11 | loop fusion | flops 14266368 | bytes 15505440 | tf_op jit(solution)/shard_map/mul | solution.py:59
  599.2 6.5 %copy.100 = f32[36,32,8,128]{3,2,1,0:T(8,128)} copy(f32[36,32,8,128]{3,1,2,0:T(8,128)S(1)} %fusion.34) | data formatting | bytes 9437184
  (405 shorter events, 270.9 us)
Async XLA Ops:
  21.4 39.4 %all-to-all-start = ((f32[3,16,512]{2,0,1:T(4,128)}), f32[3,16,512]{2,0,1:T(4,128)S(1)}, u32[]{:S(2)}, u32[]{:S(2)}) async-start(f32[3,16,512]{2,0,1:T(4,128)} %select_dynamic-update-slice_fusion), calls=%async_computation | async-start | bytes 262144 | tf_op jit(solution)/shard_map/all_to_all | solution.py:113
  64.6 46.2 %all-to-all-start.2 = ((f32[3,16,512]{2,0,1:T(4,128)}), f32[3,16,512]{2,0,1:T(4,128)S(1)}, u32[]{:S(2)}, u32[]{:S(2)}) async-start(f32[3,16,512]{2,0,1:T(4,128)} %multiply_dynamic-update-slice_fusion), calls=%async_computation.2 | async-start | bytes 262144 | tf_op jit(solution)/shard_map/all_to_all | solution.py:105
  105.0 52.0 %collective-permute-start = (f32[6,2,128]{2,1,0:T(2,128)}, f32[6,2,128]{2,1,0:T(2,128)}, u32[]{:S(2)}, u32[]{:S(2)}) collective-permute-start(f32[6,2,128]{2,1,0:T(2,128)} %get-tuple-element.82), channel_id=1, source_target_pairs={{0,2},{2,4},{4,6},{6,8},{8,10},{10,12},{12,14},{14,16},{16,18},{18... | collective-permute-start | bytes 18440 | tf_op jit(solution)/shard_map/ppermute | solution.py:21
  108.3 52.1 %collective-permute-start.1 = (f32[6,2,128]{2,1,0:T(2,128)}, f32[6,2,128]{2,1,0:T(2,128)}, u32[]{:S(2)}, u32[]{:S(2)}) collective-permute-start(f32[6,2,128]{2,1,0:T(2,128)} %get-tuple-element.81), channel_id=1, source_target_pairs={{2,0},{4,2},{6,4},{8,6},{10,8},{12,10},{14,12},{16,14},{18,16},{20... | collective-permute-start | bytes 18440 | tf_op jit(solution)/shard_map/ppermute | solution.py:22
  146.9 94.7 %collective-permute-start.21 = (f32[36,32,1,128]{3,1,2,0:T(8,128)S(1)}, f32[36,32,1,128]{3,1,2,0:T(8,128)S(1)}, u32[]{:S(2)}, u32[]{:S(2)}) collective-permute-start(f32[36,32,1,128]{3,1,2,0:T(8,128)S(1)} %get-tuple-element.67), channel_id=1, source_target_pairs={{2,0},{4,2},{6,4},{8,6},{10,8},{12,10},{14,12},{16,14},{18,16},{20... | collective-permute-start | bytes 1769480 | tf_op jit(solution)/shard_map/ppermute | solution.py:22
  151.1 90.5 %collective-permute-start.20 = (f32[36,32,1,128]{3,1,2,0:T(8,128)S(1)}, f32[36,32,1,128]{3,1,2,0:T(8,128)S(1)}, u32[]{:S(2)}, u32[]{:S(2)}) collective-permute-start(f32[36,32,1,128]{3,1,2,0:T(8,128)S(1)} %get-tuple-element.66), channel_id=1, source_target_pairs={{0,2},{2,4},{4,6},{6,8},{8,10},{10,12},{12,14},{14,16},{16,18},{18... | collective-permute-start | bytes 1769480 | tf_op jit(solution)/shard_map/ppermute | solution.py:21
  153.7 24.2 %collective-permute-start.17 = (f32[6,2,128]{2,1,0:T(2,128)S(1)}, f32[6,2,128]{2,1,0:T(2,128)S(1)}, u32[]{:S(2)}, u32[]{:S(2)}) collective-permute-start(f32[6,2,128]{2,1,0:T(2,128)S(1)} %get-tuple-element.110), channel_id=1, source_target_pairs={{2,0},{4,2},{6,4},{8,6},{10,8},{12,10},{14,12},{16,14},{18,16},{20... | collective-permute-start | bytes 18440 | tf_op jit(solution)/shard_map/ppermute | solution.py:22
  157.0 21.7 %collective-permute-start.16 = (f32[6,2,128]{2,1,0:T(2,128)S(1)}, f32[6,2,128]{2,1,0:T(2,128)S(1)}, u32[]{:S(2)}, u32[]{:S(2)}) collective-permute-start(f32[6,2,128]{2,1,0:T(2,128)S(1)} %get-tuple-element.109), channel_id=1, source_target_pairs={{0,2},{2,4},{4,6},{6,8},{8,10},{10,12},{12,14},{14,16},{16,18},{18... | collective-permute-start | bytes 18440 | tf_op jit(solution)/shard_map/ppermute | solution.py:21
  161.3 36.2 %collective-permute-start.2 = (f32[6,36,2]{2,1,0:T(8,128)S(1)}, f32[6,36,2]{2,1,0:T(8,128)S(1)}, u32[]{:S(2)}, u32[]{:S(2)}) collective-permute-start(f32[6,36,2]{2,1,0:T(8,128)S(1)} %get-tuple-element.78), channel_id=1, source_target_pairs={{0,1},{2,3},{4,5},{6,7},{8,9},{10,11},{12,13},{14,15},{16,17},{18,... | collective-permute-start | bytes 5192 | tf_op jit(solution)/shard_map/ppermute | solution.py:21
  180.2 5.1 collective-permute-start.18
  183.9 13.6 %collective-permute-start.3 = (f32[6,36,2]{2,1,0:T(8,128)S(1)}, f32[6,36,2]{2,1,0:T(8,128)S(1)}, u32[]{:S(2)}, u32[]{:S(2)}) collective-permute-start(f32[6,36,2]{2,1,0:T(8,128)S(1)} %get-tuple-element.77), channel_id=1, source_target_pairs={{1,0},{3,2},{5,4},{7,6},{9,8},{11,10},{13,12},{15,14},{17,16},{19,... | collective-permute-start | bytes 5192 | tf_op jit(solution)/shard_map/ppermute | solution.py:22
  202.3 7.1 %collective-permute-start.5 = (f32[3,2,128]{2,1,0:T(2,128)S(1)}, f32[3,2,128]{2,1,0:T(2,128)S(1)}, u32[]{:S(2)}, u32[]{:S(2)}) collective-permute-start(f32[3,2,128]{2,1,0:T(2,128)S(1)} %get-tuple-element.96), channel_id=1, source_target_pairs={{2,0},{4,2},{6,4},{8,6},{10,8},{12,10},{14,12},{16,14},{18,16},{20... | collective-permute-start | bytes 9224 | tf_op jit(solution)/shard_map/ppermute | solution.py:22
  204.7 5.6 collective-permute-start.4
  217.8 7.3 %collective-permute-start.9 = (f32[3,2,128]{2,1,0:T(2,128)S(1)}, f32[3,2,128]{2,1,0:T(2,128)S(1)}, u32[]{:S(2)}, u32[]{:S(2)}) collective-permute-start(f32[3,2,128]{2,1,0:T(2,128)S(1)} %get-tuple-element.94), channel_id=1, source_target_pairs={{2,0},{4,2},{6,4},{8,6},{10,8},{12,10},{14,12},{16,14},{18,16},{20... | collective-permute-start | bytes 9224 | tf_op jit(solution)/shard_map/ppermute | solution.py:22
  221.8 5.5 collective-permute-start.8
  234.8 93.4 %collective-permute-start.13 = (f32[3,2,128]{2,1,0:T(2,128)S(1)}, f32[3,2,128]{2,1,0:T(2,128)S(1)}, u32[]{:S(2)}, u32[]{:S(2)}) collective-permute-start(f32[3,2,128]{2,1,0:T(2,128)S(1)} %get-tuple-element.92), channel_id=1, source_target_pairs={{2,0},{4,2},{6,4},{8,6},{10,8},{12,10},{14,12},{16,14},{18,16},{20... | collective-permute-start | bytes 9224 | tf_op jit(solution)/shard_map/ppermute | solution.py:22
  239.3 89.4 %collective-permute-start.12 = (f32[3,2,128]{2,1,0:T(2,128)S(1)}, f32[3,2,128]{2,1,0:T(2,128)}, u32[]{:S(2)}, u32[]{:S(2)}) collective-permute-start(f32[3,2,128]{2,1,0:T(2,128)S(1)} %get-tuple-element.91), channel_id=1, source_target_pairs={{0,2},{2,4},{4,6},{6,8},{8,10},{10,12},{12,14},{14,16},{16,18},{18... | collective-permute-start | bytes 9224 | tf_op jit(solution)/shard_map/ppermute | solution.py:21
  253.9 25.8 %collective-permute-start.23 = (f32[36,32,10,1]{0,1,3,2:T(8,128)S(1)}, f32[36,32,10,1]{0,1,3,2:T(8,128)S(1)}, u32[]{:S(2)}, u32[]{:S(2)}) collective-permute-start(f32[36,32,10,1]{0,1,3,2:T(8,128)S(1)} %copy.86), channel_id=1, source_target_pairs={{1,0},{3,2},{5,4},{7,6},{9,8},{11,10},{13,12},{15,14},{17,16},{19,... | collective-permute-start | bytes 138248 | tf_op jit(solution)/shard_map/ppermute | solution.py:22
  260.3 25.8 %collective-permute-start.22 = (f32[36,32,10,1]{0,1,3,2:T(8,128)S(1)}, f32[36,32,10,1]{0,1,3,2:T(8,128)}, u32[]{:S(2)}, u32[]{:S(2)}) collective-permute-start(f32[36,32,10,1]{0,1,3,2:T(8,128)S(1)} %copy.84), channel_id=1, source_target_pairs={{0,1},{2,3},{4,5},{6,7},{8,9},{10,11},{12,13},{14,15},{16,17},{18,... | collective-permute-start | bytes 138248 | tf_op jit(solution)/shard_map/ppermute | solution.py:21
  319.2 19.0 %collective-permute-start.25 = (f32[36,32,1,128]{3,1,2,0:T(8,128)S(1)}, f32[36,32,1,128]{3,1,2,0:T(8,128)S(1)}, u32[]{:S(2)}, u32[]{:S(2)}) collective-permute-start(f32[36,32,1,128]{3,1,2,0:T(8,128)S(1)} %get-tuple-element.65), channel_id=1, source_target_pairs={{2,0},{4,2},{6,4},{8,6},{10,8},{12,10},{14,12},{16,14},{18,16},{20... | collective-permute-start | bytes 1769480 | tf_op jit(solution)/shard_map/ppermute | solution.py:22
  322.9 27.8 %collective-permute-start.24 = (f32[36,32,1,128]{3,1,2,0:T(8,128)S(1)}, f32[36,32,1,128]{3,1,2,0:T(8,128)S(1)}, u32[]{:S(2)}, u32[]{:S(2)}) collective-permute-start(f32[36,32,1,128]{3,1,2,0:T(8,128)S(1)} %get-tuple-element.64), channel_id=1, source_target_pairs={{0,2},{2,4},{4,6},{6,8},{8,10},{10,12},{12,14},{14,16},{16,18},{18... | collective-permute-start | bytes 1769480 | tf_op jit(solution)/shard_map/ppermute | solution.py:21
  362.9 19.0 %collective-permute-start.27 = (f32[36,32,10,1]{0,1,3,2:T(8,128)S(1)}, f32[36,32,10,1]{0,1,3,2:T(8,128)S(1)}, u32[]{:S(2)}, u32[]{:S(2)}) collective-permute-start(f32[36,32,10,1]{0,1,3,2:T(8,128)S(1)} %copy.90), channel_id=1, source_target_pairs={{1,0},{3,2},{5,4},{7,6},{9,8},{11,10},{13,12},{15,14},{17,16},{19,... | collective-permute-start | bytes 138248 | tf_op jit(solution)/shard_map/ppermute | solution.py:22
  369.3 19.0 %collective-permute-start.26 = (f32[36,32,10,1]{0,1,3,2:T(8,128)S(1)}, f32[36,32,10,1]{0,1,3,2:T(8,128)}, u32[]{:S(2)}, u32[]{:S(2)}) collective-permute-start(f32[36,32,10,1]{0,1,3,2:T(8,128)S(1)} %copy.88), channel_id=1, source_target_pairs={{0,1},{2,3},{4,5},{6,7},{8,9},{10,11},{12,13},{14,15},{16,17},{18,... | collective-permute-start | bytes 138248 | tf_op jit(solution)/shard_map/ppermute | solution.py:21
  415.3 19.0 %collective-permute-start.29 = (f32[36,32,1,128]{3,1,2,0:T(8,128)S(1)}, f32[36,32,1,128]{3,1,2,0:T(8,128)S(1)}, u32[]{:S(2)}, u32[]{:S(2)}) collective-permute-start(f32[36,32,1,128]{3,1,2,0:T(8,128)S(1)} %get-tuple-element.63), channel_id=1, source_target_pairs={{2,0},{4,2},{6,4},{8,6},{10,8},{12,10},{14,12},{16,14},{18,16},{20... | collective-permute-start | bytes 1769480 | tf_op jit(solution)/shard_map/ppermute | solution.py:22
  417.2 25.4 %collective-permute-start.28 = (f32[36,32,1,128]{3,1,2,0:T(8,128)S(1)}, f32[36,32,1,128]{3,1,2,0:T(8,128)S(1)}, u32[]{:S(2)}, u32[]{:S(2)}) collective-permute-start(f32[36,32,1,128]{3,1,2,0:T(8,128)S(1)} %get-tuple-element.62), channel_id=1, source_target_pairs={{0,2},{2,4},{4,6},{6,8},{8,10},{10,12},{12,14},{14,16},{16,18},{18... | collective-permute-start | bytes 1769480 | tf_op jit(solution)/shard_map/ppermute | solution.py:21
  422.1 5.5 collective-permute-start.15
  454.8 18.9 %collective-permute-start.31 = (f32[36,32,10,1]{0,1,3,2:T(8,128)S(1)}, f32[36,32,10,1]{0,1,3,2:T(8,128)S(1)}, u32[]{:S(2)}, u32[]{:S(2)}) collective-permute-start(f32[36,32,10,1]{0,1,3,2:T(8,128)S(1)} %copy.94), channel_id=1, source_target_pairs={{1,0},{3,2},{5,4},{7,6},{9,8},{11,10},{13,12},{15,14},{17,16},{19,... | collective-permute-start | bytes 138248 | tf_op jit(solution)/shard_map/ppermute | solution.py:22
  461.1 18.9 %collective-permute-start.30 = (f32[36,32,10,1]{0,1,3,2:T(8,128)S(1)}, f32[36,32,10,1]{0,1,3,2:T(8,128)}, u32[]{:S(2)}, u32[]{:S(2)}) collective-permute-start(f32[36,32,10,1]{0,1,3,2:T(8,128)S(1)} %copy.92), channel_id=1, source_target_pairs={{0,1},{2,3},{4,5},{6,7},{8,9},{10,11},{12,13},{14,15},{16,17},{18,... | collective-permute-start | bytes 138248 | tf_op jit(solution)/shard_map/ppermute | solution.py:21
  507.1 19.0 %collective-permute-start.33 = (f32[36,32,1,128]{3,1,2,0:T(8,128)S(1)}, f32[36,32,1,128]{3,1,2,0:T(8,128)S(1)}, u32[]{:S(2)}, u32[]{:S(2)}) collective-permute-start(f32[36,32,1,128]{3,1,2,0:T(8,128)S(1)} %get-tuple-element.61), channel_id=1, source_target_pairs={{2,0},{4,2},{6,4},{8,6},{10,8},{12,10},{14,12},{16,14},{18,16},{20... | collective-permute-start | bytes 1769480 | tf_op jit(solution)/shard_map/ppermute | solution.py:22
  509.1 29.5 %collective-permute-start.32 = (f32[36,32,1,128]{3,1,2,0:T(8,128)S(1)}, f32[36,32,1,128]{3,1,2,0:T(8,128)S(1)}, u32[]{:S(2)}, u32[]{:S(2)}) collective-permute-start(f32[36,32,1,128]{3,1,2,0:T(8,128)S(1)} %get-tuple-element.60), channel_id=1, source_target_pairs={{0,2},{2,4},{4,6},{6,8},{8,10},{10,12},{12,14},{14,16},{16,18},{18... | collective-permute-start | bytes 1769480 | tf_op jit(solution)/shard_map/ppermute | solution.py:21
  550.8 18.3 %collective-permute-start.35 = (f32[36,32,10,1]{0,1,3,2:T(8,128)S(1)}, f32[36,32,10,1]{0,1,3,2:T(8,128)S(1)}, u32[]{:S(2)}, u32[]{:S(2)}) collective-permute-start(f32[36,32,10,1]{0,1,3,2:T(8,128)S(1)} %copy.98), channel_id=1, source_target_pairs={{1,0},{3,2},{5,4},{7,6},{9,8},{11,10},{13,12},{15,14},{17,16},{19,... | collective-permute-start | bytes 138248 | tf_op jit(solution)/shard_map/ppermute | solution.py:22
  557.1 18.2 %collective-permute-start.34 = (f32[36,32,10,1]{0,1,3,2:T(8,128)S(1)}, f32[36,32,10,1]{0,1,3,2:T(8,128)S(1)}, u32[]{:S(2)}, u32[]{:S(2)}) collective-permute-start(f32[36,32,10,1]{0,1,3,2:T(8,128)S(1)} %copy.96), channel_id=1, source_target_pairs={{0,1},{2,3},{4,5},{6,7},{8,9},{10,11},{12,13},{14,15},{16,17},{18,... | collective-permute-start | bytes 138248 | tf_op jit(solution)/shard_map/ppermute | solution.py:21
  (102 other events, 1710.0 us)
where the time goes:
time: 616 us; the launch traced here: 606 us
  other arithmetic  224 us (36%)
  local copies, waits for them, and re-layouts  178 us (29%)
  starting transfers between devices  115 us (19%)
  waiting for transfers between devices  77.5 us (13%)
  blocking collectives  7.67 us (1%)
    ppermute x18, starting transfers between devices, padded_2(): before = lax.ppermute(last, axis, up)  60.9 us
    mul x4, other arithmetic, advect(): (jnp.maximum(face_y, 0.0) * padded[:, :, 1:-1, :-1] + jnp.minimum(face_y,...  53.9 us
    slice x17, local copies, waits for them, and re-layouts, padded_2(): last = lax.slice_in_dim(value, length - width, length, axis=dim)  46.8 us
    mul x4, other arithmetic, advect(): (jnp.maximum(face_x, 0.0) * padded[:, :, :-1, 1:-1] + jnp.minimum(face_x,...  41.5 us
    ppermute x18, starting transfers between devices, padded_2(): after = lax.ppermute(initial, axis, down)  40 us
    ppermute x18, waiting for transfers between devices, padded_2(): before = lax.ppermute(last, axis, up)  38.8 us
    ppermute x18, waiting for transfers between devices, padded_2(): after = lax.ppermute(initial, axis, down)  38.7 us
    ppermute x4, local copies, waits for them, and re-layouts, padded_2(): before = lax.ppermute(last, axis, up)  28 us
  transfers between devices with their start and end apart: 38, of which 12 were waited for; matrix products, arithmetic and copies ran while one was open for 43% of the time, Pallas kernels for 0%

commit v1 on v0

--- a/solution.py
+++ b/solution.py
@@ -3,6 +3,8 @@
 import jax
 import jax.numpy as jnp
 from jax import lax
+from jax.experimental import pallas as pl
+from jax.experimental.pallas import tpu as pltpu
 from jax.sharding import PartitionSpec as P
 
 ND = 36
@@ -89,35 +91,206 @@
     return (slope_x, slope_y)
 
 
-def route_blocks(blocks, toward_waves):
-    tile_count = lax.axis_size("tile")
-    col_count = lax.axis_size("col")
-    peer_count = blocks.shape[1]
-    slot_count = blocks.shape[2]
-    tile_index = lax.axis_index("tile")
-    col_index = lax.axis_index("col")
-    anchor = jnp.zeros((), jnp.int32)
-    spread = jnp.zeros((3, tile_count, slot_count), jnp.float32)
-    spread = lax.dynamic_update_slice(spread, blocks, (anchor, col_index * peer_count, anchor))
-    flattened = spread.reshape(3, tile_count * slot_count)
-    if toward_waves:
-        delivered = lax.all_to_all(
-            lax.all_to_all(flattened, "tile", split_axis=1, concat_axis=1, tiled=True),
-            "col",
-            split_axis=1,
-            concat_axis=1,
-            tiled=True,
-        )
-    else:
-        delivered = lax.all_to_all(
-            lax.all_to_all(flattened, "tile", split_axis=1, concat_axis=1, tiled=True),
-            "col",
-            split_axis=1,
-            concat_axis=1,
-            tiled=True,
-        )
-    delivered = delivered.reshape(3, col_count, peer_count, slot_count)
-    return lax.dynamic_index_in_dim(delivered, tile_index // peer_count, 1, keepdims=False)
+def split_parts(x):
+    high = x.astype(jnp.bfloat16).astype(jnp.float32)
+    rest = x - high
+    middle = rest.astype(jnp.bfloat16).astype(jnp.float32)
+    low = rest - middle
+    return jnp.concatenate([high, middle, low], axis=0).astype(jnp.bfloat16)
+
+
+def join_parts(r):
+    return r[0:8] + r[8:16] + r[16:24]
+
+
+def block_onehot(source_row, j, row_length, width):
+    cells = source_row.shape[1]
+    n = lax.broadcasted_iota(jnp.int32, (cells, cells), 0)
+    ids = (n // width) * row_length + j * width + n % width
+    return jnp.where(ids == source_row, 1.0, 0.0).astype(jnp.bfloat16)
+
+
+def wave_onehot(target_row, cells):
+    n = lax.broadcasted_iota(jnp.int32, (cells, target_row.shape[1]), 0)
+    return jnp.where(n == target_row, 1.0, 0.0).astype(jnp.bfloat16)
+
+
+NN = (((1,), (0,)), ((), ()))
+NT = (((1,), (1,)), ((), ()))
+
+
+def gather_kernel(row_length, width, spectra, wet, surface, source, target, weight, out, flat):
+    span_x, span_y = wet.shape
+    peers = source.shape[0]
+    zero = jnp.zeros((span_x, span_y), jnp.float32)
+    acc = [zero, zero, zero]
+    for d in range(ND):
+        theta = (d + 0.5) * (2.0 * math.pi / ND)
+        part = jnp.sum(spectra[d], axis=0)
+        cos, sin = math.cos(theta), math.sin(theta)
+        for c, m in enumerate((cos * cos, cos * sin, sin * sin)):
+            acc[c] = acc[c] + part * (m * 0.5 / (ND * NF))
+    wetf = wet[...].astype(jnp.float32)
+    flat[...] = jnp.zeros_like(flat)
+    for c in range(3):
+        plane = acc[c] * wetf
+        for x in range(span_x):
+            flat[3 + c : 4 + c, x * span_y : (x + 1) * span_y] = plane[x : x + 1, :]
+    stress = split_parts(flat[...])
+
+    def step(j, carry):
+        hot = block_onehot(source[j], j, row_length, width)
+        values = join_parts(
+            lax.dot_general(split_parts(surface[j]), hot, NN, preferred_element_type=jnp.float32)
+        )
+        hot2 = wave_onehot(target[j], span_x * span_y)
+        back = join_parts(
+            lax.dot_general(stress, hot2, NN, preferred_element_type=jnp.float32)
+        )
+        out[j] = values * weight[j] + back
+        return carry
+
+    lax.fori_loop(0, peers, step, 0)
+
+
+def swap_kernel(src, dst, send_sem, recv_sem, local_sem):
+    peers = src.shape[0]
+    t = lax.axis_index("tile")
+    c = lax.axis_index("col")
+    side = t // peers
+    slot = lax.rem(t, peers)
+    barrier = pltpu.get_barrier_semaphore()
+
+    def partner(j):
+        return {"tile": c * peers + j, "col": side}
+
+    def copy(j):
+        return pltpu.make_async_remote_copy(
+            src_ref=src.at[j],
+            dst_ref=dst.at[slot],
+            send_sem=send_sem.at[j],
+            recv_sem=recv_sem.at[slot],
+            device_id=partner(j),
+            device_id_type=pl.DeviceIdType.MESH,
+        )
+
+    def arrival(j):
+        return pltpu.make_async_remote_copy(
+            src_ref=src.at[j],
+            dst_ref=dst.at[j],
+            send_sem=send_sem.at[j],
+            recv_sem=recv_sem.at[j],
+            device_id=partner(j),
+            device_id_type=pl.DeviceIdType.MESH,
+        )
+
+    def other(j):
+        return jnp.logical_or(side != c, slot != j)
+
+    for j in range(peers):
+
+        @pl.when(other(j))
+        def _():
+            pl.semaphore_signal(
+                barrier, inc=1, device_id=partner(j), device_id_type=pl.DeviceIdType.MESH
+            )
+
+    @pl.when(side == c)
+    def _():
+        pl.semaphore_wait(barrier, peers - 1)
+
+    @pl.when(side != c)
+    def _():
+        pl.semaphore_wait(barrier, peers)
+
+    for j in range(peers):
+
+        @pl.when(other(j))
+        def _():
+            copy(j).start()
+
+        @pl.when(jnp.logical_not(other(j)))
+        def _():
+            own = pltpu.make_async_copy(src.at[j], dst.at[j], local_sem)
+            own.start()
+            own.wait()
+
+    for j in range(peers):
+
+        @pl.when(other(j))
+        def _():
+            copy(j).wait_send()
+            arrival(j).wait_recv()
+
+
+def scatter_kernel(row_length, width, arrived, source, target, waves, ocean):
+    peers = source.shape[0]
+    waves[...] = jnp.zeros_like(waves)
+
+    def step(j, carry):
+        parts = split_parts(arrived[j])
+        hot = block_onehot(source[j], j, row_length, width)
+        ocean[j] = join_parts(
+            lax.dot_general(parts, hot, NT, preferred_element_type=jnp.float32)
+        )
+        hot2 = wave_onehot(target[j], waves.shape[1])
+        waves[...] += join_parts(
+            lax.dot_general(parts, hot2, NT, preferred_element_type=jnp.float32)
+        )
+        return carry
+
+    lax.fori_loop(0, peers, step, 0)
+
+
+VMEM = pl.BlockSpec(memory_space=pltpu.VMEM)
+
+
+def remap(spectra, wave_wet, surface, remap_source, remap_target, remap_weight):
+    peers, slots = remap_source.shape[1:]
+    span_x, span_y = wave_wet.shape
+    rows, cols = surface.shape[1:]
+    width = cols // peers
+    source = remap_source.reshape(peers, 1, slots)
+    target = remap_target.reshape(peers, 1, slots)
+    weight = remap_weight.reshape(peers, 1, slots)
+    blocks = surface.reshape(3, rows, peers, width).transpose(2, 0, 1, 3).reshape(peers, 3, slots)
+    blocks = jnp.concatenate([blocks, jnp.zeros((peers, 5, slots), jnp.float32)], axis=1)
+    shape = jax.ShapeDtypeStruct((peers, 8, slots), jnp.float32)
+    sent = pl.pallas_call(
+        lambda *refs: gather_kernel(cols, width, *refs),
+        out_shape=shape,
+        in_specs=[VMEM] * 6,
+        out_specs=VMEM,
+        scratch_shapes=[pltpu.VMEM((8, span_x * span_y), jnp.float32)],
+        compiler_params=pltpu.CompilerParams(vmem_limit_bytes=32 * 1024 * 1024),
+    )(spectra, wave_wet, blocks, source, target, weight)
+    arrived = pl.pallas_call(
+        swap_kernel,
+        out_shape=shape,
+        in_specs=[VMEM],
+        out_specs=VMEM,
+        scratch_shapes=[
+            pltpu.SemaphoreType.DMA((peers,)),
+            pltpu.SemaphoreType.DMA((peers,)),
+            pltpu.SemaphoreType.DMA,
+        ],
+        compiler_params=pltpu.CompilerParams(collective_id=0, has_side_effects=True),
+    )(sent)
+    waves, ocean = pl.pallas_call(
+        lambda *refs: scatter_kernel(cols, width, *refs),
+        out_shape=(jax.ShapeDtypeStruct((8, span_x * span_y), jnp.float32), shape),
+        in_specs=[VMEM] * 3,
+        out_specs=(VMEM, VMEM),
+        compiler_params=pltpu.CompilerParams(vmem_limit_bytes=32 * 1024 * 1024),
+    )(arrived, source, target)
+    currents = waves[:3].reshape(3, span_x, span_y)
+    ocean_stress = (
+        ocean[:, 3:6]
+        .reshape(peers, 3, rows, width)
+        .transpose(1, 2, 0, 3)
+        .reshape(3, rows, cols)
+    )
+    return currents, ocean_stress
 
 
 def body(
@@ -139,38 +312,16 @@
     tile_count = lax.axis_size("tile")
     col_count = lax.axis_size("col")
     tile_rows, tile_cols = surface_height.shape
-    span_x, span_y = wave_wet.shape
-    peer_count = remap_source.shape[1]
-    slot_count = remap_source.shape[2]
     sea_cells = ocean_wet.astype(jnp.float32)
     wet_cells = wave_wet.astype(jnp.float32)
     zonal_flow = zonal_velocity * sea_cells[None]
     meridional = meridional_velocity * sea_cells[None]
     height = surface_height
     energy = spectra * wet_cells[None, None]
-    sources = remap_source[0].reshape(peer_count * slot_count)
-    targets = remap_target[0].reshape(peer_count * slot_count)
-    weights = remap_weight[0]
-    surface = jnp.stack([zonal_flow[0], meridional[0], height]).reshape(3, tile_rows * tile_cols)
-    surface = jnp.concatenate([surface, jnp.zeros((3, 1), jnp.float32)], axis=1)
-    outgoing = jnp.take(surface, sources, axis=1).reshape(3, peer_count, slot_count) * weights[None]
-    arrived = route_blocks(outgoing, True)
-    currents = (
-        jnp.zeros((3, span_x * span_y + 1), jnp.float32)
-        .at[:, targets]
-        .add(arrived.reshape(3, peer_count * slot_count))
-    )
-    currents = currents[:, :-1].reshape(3, span_x, span_y)
-    stress = radiation_stress(energy, tables).reshape(3, span_x * span_y)
-    stress = jnp.concatenate([stress, jnp.zeros((3, 1), jnp.float32)], axis=1)
-    returning = jnp.take(stress, targets, axis=1).reshape(3, peer_count, slot_count)
-    returned = route_blocks(returning, False)
-    ocean_stress = (
-        jnp.zeros((3, tile_rows * tile_cols + 1), jnp.float32)
-        .at[:, sources]
-        .add(returned.reshape(3, peer_count * slot_count))
-    )
-    ocean_stress = ocean_stress[:, :-1].reshape(3, tile_rows, tile_cols)
+    surface = jnp.stack([zonal_flow[0], meridional[0], height])
+    currents, ocean_stress = remap(
+        spectra, wave_wet, surface, remap_source, remap_target, remap_weight
+    )
     fields = jnp.stack(
         [
             0.03 * currents[0],

time: 616 us -> 634 us (1.029)
  other arithmetic: 224 us -> 265 us
  waiting for transfers between devices: 77.5 us -> 47.7 us
  Pallas kernels: 0 us -> 16.9 us
  starting transfers between devices: 115 us -> 103 us
  local copies, waits for them, and re-layouts: 178 us -> 189 us
  blocking collectives: 7.67 us -> 0 us
    scatter-add x2 -> x0, other arithmetic: 49.9 us -> none  [the longest x1 25.4 us: body(): ocean_stress = jnp.zeros((3, tile_rows * tile_cols + 1), jnp.float32).at[...]
    reduce_sum x4, other arithmetic: 3.43 us -> 36.4 us  [body(): jnp.sum(thickness[:, None, None] * zonal_flow, axis=0) / column_depth]
    gather x4 -> x0, local copies, waits for them, and re-layouts: 29.3 us -> none  [the longest x2 18 us: body(): jnp.take(surface, sources, axis=1).reshape(3, peer_count, slot_count)]
    unnamed x203 -> x211, local copies, waits for them, and re-layouts: 11.8 us -> 40.5 us
    ppermute x18, waiting for transfers between devices: 38.7 us -> 11.7 us  [padded_2(): after = lax.ppermute(initial, axis, down)]
    mul x4, other arithmetic: 3.18 us -> 30.1 us  [mixing_tendency(): interface_flux = mixing[1:, None, None] * (profile[:-1] - profile[1:])]
    pallas_call x0 -> x3, Pallas kernels: none -> 16.9 us  [the longest x1 8.93 us: remap(): pl.pallas_call(swap_kernel, out_shape=shape, in_specs=[VMEM], out_specs=V...]
    all_to_all x2 -> x0, starting transfers between devices: 14 us -> none  [route_blocks(): lax.all_to_all(flattened, 'tile', split_axis=1, concat_axis=1, tiled=True)]
  transfers between devices with their start and end apart: 38 -> 36, of which waited for: 12 -> 6; matrix products, arithmetic and copies ran while one was open for 43% -> 52% of each run, Pallas kernels for 0% -> 0%
where the time goes in v1:
time: 634 us; the launch traced here: 624 us
  other arithmetic  265 us (42%)
  local copies, waits for them, and re-layouts  189 us (30%)
  starting transfers between devices  103 us (16%)
  waiting for transfers between devices  47.7 us (8%)
  Pallas kernels  16.9 us (3%)
    ppermute x18, starting transfers between devices, padded_2(): before = lax.ppermute(last, axis, up)  63.2 us
    slice x17, local copies, waits for them, and re-layouts, padded_2(): last = lax.slice_in_dim(value, length - width, length, axis=dim)  54.1 us
    mul x4, other arithmetic, advect(): (jnp.maximum(face_y, 0.0) * padded[:, :, 1:-1, :-1] + jnp.minimum(face_y,...  53.4 us
    mul x4, other arithmetic, advect(): (jnp.maximum(face_x, 0.0) * padded[:, :, :-1, 1:-1] + jnp.minimum(face_x,...  42.6 us
    unnamed x211, local copies, waits for them, and re-layouts  40.5 us
    ppermute x18, starting transfers between devices, padded_2(): after = lax.ppermute(initial, axis, down)  40 us
    reduce_sum x4, other arithmetic, body(): jnp.sum(thickness[:, None, None] * zonal_flow, axis=0) / column_depth  36.4 us
    ppermute x18, waiting for transfers between devices, padded_2(): before = lax.ppermute(last, axis, up)  36 us
  transfers between devices with their start and end apart: 36, of which 6 were waited for; matrix products, arithmetic and copies ran while one was open for 52% of the time, Pallas kernels for 0%

profile of v1, /device:TPU:18, one launch (start us, length us, event | category | flops | bytes accessed | tf_op | source)
XLA Modules:
  0.0 624.4 jit_solution(2253095815487364815)
XLA Ops:
  27.1 8.9 %shard_map.157.refs_0_ = f32[8,8,512]{2,1,0:T(8,128)} custom-call(f32[8,8,512]{2,1,0:T(8,128)} %copy-done.1), custom_call_target="tpu_custom_call" | custom-call | tf_op jit(solution)/shard_map/pallas_call | solution.py:267
  80.0 7.0 %fusion.82 = (f32[49,32,128]{1,2,0:T(8,128)}, f32[49,32,128]{1,2,0:T(8,128)}) fusion(f32[50,32,128]{1,2,0:T(8,128)S(1)} %get-tuple-element.52, f32[49]{0:T(128)S(1)} %slice.608, f32[50,32,128]{1,2,0:T(8,128)} %copy-done.8), kind=kLoop, calls=%fused_computation.159 | loop fusion | flops 802816 | bytes 4817092 | tf_op jit(solution)/shard_map/mul | solution.py:82
  128.3 11.6 %multiply_reduce_fusion.5 = (f32[32,128]{0,1:T(8,128)}, f32[32,128]{0,1:T(8,128)S(1)}, f32[50,32,128]{1,2,0:T(8,128)}, f32[50,32,128]{1,2,0:T(8,128)}) fusion(f32[50]{0:T(128)S(1)} %copy-done.81, f32[32,128]{0,1:T(8,128)S(1)} %copy-done.24, f32[1,32,128]{1,2,0:T(8,128)} %get-tuple-element.74, f32[49,32,128]{1,2,0:T(8,128)} %get-tuple-element.128, ...), kind=kLoop, calls=%fused_computation.141 | loop fusion | flops 4497408 | bytes 5030216 | tf_op jit(solution)/shard_map/reduce_sum | solution.py:358
  149.1 9.7 %fusion.80 = (f32[49,32,128]{1,2,0:T(8,128)}, f32[49,32,128]{1,2,0:T(8,128)}) fusion(f32[50,32,128]{1,2,0:T(8,128)} %get-tuple-element.51, f32[49]{0:T(128)S(1)} %copy-done.86, f32[50,32,128]{1,2,0:T(8,128)} %get-tuple-element.50), kind=kLoop, calls=%fused_computation.155 | loop fusion | flops 802816 | bytes 4817092 | tf_op jit(solution)/shard_map/mul | solution.py:82
  170.7 10.0 %multiply_reduce_fusion.3 = (f32[32,128]{0,1:T(8,128)}, f32[32,128]{0,1:T(8,128)S(1)}, f32[50,32,128]{1,2,0:T(8,128)}, f32[50,32,128]{1,2,0:T(8,128)}) fusion(f32[50]{0:T(128)} %param.16, f32[32,128]{0,1:T(8,128)S(1)} %copy-done.25, f32[1,32,128]{1,2,0:T(8,128)} %slice_multiply_fusion.4, f32[49,32,128]{1,2,0:T(8,128)} %get-tuple-element.126, ...), kind=kLoop, calls=%fused_computation.139 | loop fusion | flops 4497408 | bytes 5030216 | tf_op jit(solution)/shard_map/reduce_sum | solution.py:358
  189.8 9.8 %fusion.78 = (f32[49,32,128]{1,2,0:T(8,128)}, f32[49,32,128]{1,2,0:T(8,128)}) fusion(f32[50,32,128]{1,2,0:T(8,128)} %get-tuple-element.49, f32[49]{0:T(128)S(1)} %copy-done.87, f32[50,32,128]{1,2,0:T(8,128)} %get-tuple-element.48), kind=kLoop, calls=%fused_computation.151 | loop fusion | flops 802816 | bytes 4817092 | tf_op jit(solution)/shard_map/mul | solution.py:82
  210.3 10.1 %multiply_reduce_fusion.1 = (f32[32,128]{0,1:T(8,128)}, f32[32,128]{0,1:T(8,128)}, f32[50,32,128]{1,2,0:T(8,128)}, f32[50,32,128]{1,2,0:T(8,128)}) fusion(f32[50]{0:T(128)} %param.16, f32[32,128]{0,1:T(8,128)S(1)} %copy-done.25, f32[1,32,128]{1,2,0:T(8,128)} %slice_multiply_fusion.2, f32[49,32,128]{1,2,0:T(8,128)} %get-tuple-element.124, ...), kind=kLoop, calls=%fused_computation.137 | loop fusion | flops 4497408 | bytes 5030216 | tf_op jit(solution)/shard_map/reduce_sum | solution.py:358
  234.7 6.6 %fusion.135 = (f32[36,32,10,1]{3,1,2,0:T(8,128)}, f32[36,32,10,1]{3,1,2,0:T(8,128)}) fusion(f32[36,32,10,128]{3,1,2,0:T(8,128)S(1)} %pad_maximum_fusion.32), kind=kLoop, calls=%fused_computation.313 | loop fusion | bytes 184320 | tf_op jit(solution)/shard_map/slice | solution.py:21
  255.9 15.8 %fusion.19 = (f32[36,32,9,128]{3,1,2,0:T(8,128)}, f32[36,32,9,128]{3,1,2,0:T(8,128)}) fusion(f32[36,32,8,128]{3,1,2,0:T(8,128)} %copy-done.7, f32[36,32,1,128]{3,1,2,0:T(8,128)} %collective-permute-done.20, f32[36,32,1,128]{3,1,2,0:T(8,128)} %collective-permute-done.21, f32[9,128]{1,0:T(8,128)S(1)} %copy-done.41, f32[36,32,10,130]{3,1,2,0:T(8,128)} %broadcast_add_fusion.1), kind=kLoop, calls=%fused_computation.64 | loop fusion | flops 13271040 | bytes 27136512 | tf_op jit(solution)/shard_map/mul | solution.py:55
  271.8 6.3 %copy.241 = f32[36,32,10,1]{3,1,2,0:T(8,128)} copy(f32[36,32,10,1]{0,1,3,2:T(8,128)S(1)} %collective-permute-done.23) | data formatting | bytes 92160 | tf_op jit(solution)/shard_map/ppermute | solution.py:24
  284.4 17.6 %fusion.14 = (f32[36,32,8,129]{3,1,2,0:T(8,128)S(1)}, f32[36,32,8,129]{3,1,2,0:T(8,128)}) fusion(f32[36,32,10,1]{3,1,2,0:T(8,128)} %copy.241, f32[36,32,1,128]{3,1,2,0:T(8,128)} %collective-permute-done.21, f32[36,32,8,128]{3,1,2,0:T(8,128)} %copy-done.7, f32[36,32,1,128]{3,1,2,0:T(8,128)} %collective-permute-done.20, f32[36,32,10,1]{3,1,2,0:T(8,128)} %copy.239, ...), kind=kLoop, calls=%fused_computation.37 | loop fusion | flops 16644096 | bytes 25016352 | tf_op jit(solution)/shard_map/mul | solution.py:61
  334.3 15.7 %collective-permute-done.24 = f32[36,32,1,128]{3,1,2,0:T(8,128)} collective-permute-done((f32[36,32,1,128]{3,1,2,0:T(8,128)}, f32[36,32,1,128]{3,1,2,0:T(8,128)}, u32[]{:S(2)}, u32[]{:S(2)}) %collective-permute-start.24) | collective-permute-done | bytes 589856 | tf_op jit(solution)/shard_map/ppermute | solution.py:23
  353.4 6.6 %fusion.134 = (f32[36,32,10,1]{3,1,2,0:T(8,128)}, f32[36,32,10,1]{3,1,2,0:T(8,128)}) fusion(f32[36,32,10,128]{3,1,2,0:T(8,128)S(1)} %pad_maximum_fusion.33), kind=kLoop, calls=%fused_computation.312 | loop fusion | bytes 184320 | tf_op jit(solution)/shard_map/slice | solution.py:21
  377.0 8.9 %fusion.21 = f32[36,32,9,128]{3,1,2,0:T(8,128)} fusion(f32[36,32,8,128]{3,1,2,0:T(8,128)} %copy-done.4, f32[36,32,1,128]{3,1,2,0:T(8,128)} %collective-permute-done.24, f32[36,32,1,128]{3,1,2,0:T(8,128)} %collective-permute-done.25, f32[36,32,9,128]{3,1,2,0:T(8,128)} %get-tuple-element.39, f32[9,128]{1,0:T(8,128)S(1)} %copy-done.42), kind=kLoop, calls=%fused_computation.68 | loop fusion | flops 10616832 | bytes 16519680 | tf_op jit(solution)/shard_map/mul | solution.py:55
  385.9 7.2 %copy.245 = f32[36,32,10,1]{3,1,2,0:T(8,128)} copy(f32[36,32,10,1]{0,1,3,2:T(8,128)} %collective-permute-done.27) | data formatting | bytes 92160 | tf_op jit(solution)/shard_map/ppermute | solution.py:24
  393.1 7.2 %copy.243 = f32[36,32,10,1]{3,1,2,0:T(8,128)} copy(f32[36,32,10,1]{0,1,3,2:T(8,128)} %collective-permute-done.26) | data formatting | bytes 92160 | tf_op jit(solution)/shard_map/ppermute | solution.py:23
  400.3 11.9 %fusion.10 = f32[36,32,8,129]{3,1,2,0:T(8,128)S(1)} fusion(f32[36,32,10,1]{3,1,2,0:T(8,128)} %copy.245, f32[36,32,1,128]{3,1,2,0:T(8,128)} %collective-permute-done.25, f32[36,32,8,128]{3,1,2,0:T(8,128)} %copy-done.4, f32[36,32,1,128]{3,1,2,0:T(8,128)} %collective-permute-done.24, f32[36,32,10,1]{3,1,2,0:T(8,128)} %copy.243, ...), kind=kLoop, calls=%fused_computation.27 | loop fusion | flops 14266368 | bytes 15505440 | tf_op jit(solution)/shard_map/mul | solution.py:61
  412.2 6.7 %fusion.120 = (f32[8,128]{1,0:T(8,128)S(1)}, f32[36,32,8,128]{3,1,2,0:T(8,128)S(1)}) fusion(f32[36,32,8,129]{3,1,2,0:T(8,128)S(1)} %fusion.10, f32[36,32,9,128]{3,1,2,0:T(8,128)} %fusion.21, f32[36,32,8,128]{3,1,2,0:T(8,128)} %copy-done.14, f32[8,128]{1,0:T(8,128)S(1)} %copy-done.72, f32[32]{0:T(128)S(1)} %copy-done.75, ...), kind=kLoop, calls=%fused_computation.308 | loop fusion | flops 9436160 | bytes 28467328 | tf_op jit(solution)/shard_map/reduce_sum | solution.py:41
  430.8 9.3 %collective-permute-done.29 = f32[36,32,1,128]{3,1,2,0:T(8,128)S(1)} collective-permute-done((f32[36,32,1,128]{3,1,2,0:T(8,128)S(1)}, f32[36,32,1,128]{3,1,2,0:T(8,128)S(1)}, u32[]{:S(2)}, u32[]{:S(2)}) %collective-permute-start.29) | collective-permute-done | bytes 589856 | tf_op jit(solution)/shard_map/ppermute | solution.py:24
  440.1 7.3 %collective-permute-done.28 = f32[36,32,1,128]{3,1,2,0:T(8,128)S(1)} collective-permute-done((f32[36,32,1,128]{3,1,2,0:T(8,128)S(1)}, f32[36,32,1,128]{3,1,2,0:T(8,128)S(1)}, u32[]{:S(2)}, u32[]{:S(2)}) %collective-permute-start.28) | collective-permute-done | bytes 589856 | tf_op jit(solution)/shard_map/ppermute | solution.py:23
  448.9 6.6 %fusion.133 = (f32[36,32,10,1]{3,1,2,0:T(8,128)}, f32[36,32,10,1]{3,1,2,0:T(8,128)}) fusion(f32[36,32,10,128]{3,1,2,0:T(8,128)S(1)} %pad_maximum_fusion.34), kind=kLoop, calls=%fused_computation.311 | loop fusion | bytes 184320 | tf_op jit(solution)/shard_map/slice | solution.py:21
  472.7 8.9 %fusion.23 = f32[36,32,9,128]{3,1,2,0:T(8,128)} fusion(f32[36,32,8,128]{3,1,2,0:T(8,128)} %copy-done.6, f32[36,32,1,128]{3,1,2,0:T(8,128)} %copy-done.21, f32[36,32,1,128]{3,1,2,0:T(8,128)} %copy-done.20, f32[36,32,9,128]{3,1,2,0:T(8,128)} %get-tuple-element.39, f32[9,128]{1,0:T(8,128)S(1)} %copy-done.42), kind=kLoop, calls=%fused_computation.72 | loop fusion | flops 10616832 | bytes 16519680 | tf_op jit(solution)/shard_map/mul | solution.py:55
  481.6 7.2 %copy.249 = f32[36,32,10,1]{3,1,2,0:T(8,128)} copy(f32[36,32,10,1]{0,1,3,2:T(8,128)} %collective-permute-done.31) | data formatting | bytes 92160 | tf_op jit(solution)/shard_map/ppermute | solution.py:24
  488.8 7.2 %copy.247 = f32[36,32,10,1]{3,1,2,0:T(8,128)} copy(f32[36,32,10,1]{0,1,3,2:T(8,128)} %collective-permute-done.30) | data formatting | bytes 92160 | tf_op jit(solution)/shard_map/ppermute | solution.py:23
  496.0 11.8 %fusion.6 = f32[36,32,8,129]{3,1,2,0:T(8,128)S(1)} fusion(f32[36,32,10,1]{3,1,2,0:T(8,128)} %copy.249, f32[36,32,1,128]{3,1,2,0:T(8,128)} %copy-done.20, f32[36,32,8,128]{3,1,2,0:T(8,128)} %copy-done.6, f32[36,32,1,128]{3,1,2,0:T(8,128)} %copy-done.21, f32[36,32,10,1]{3,1,2,0:T(8,128)} %copy.247, f32[36,32,8,129]{3,1,2,0:T(8,128)} %get-tuple-element.41, ...), kind=kLoop, calls=%fused_computation.17 | loop fusion | flops 14266368 | bytes 15505440 | tf_op jit(solution)/shard_map/mul | solution.py:61
  507.9 6.7 %fusion.118 = (f32[8,128]{1,0:T(8,128)S(1)}, f32[36,32,8,128]{3,1,2,0:T(8,128)S(1)}) fusion(f32[36,32,8,129]{3,1,2,0:T(8,128)S(1)} %fusion.6, f32[36,32,9,128]{3,1,2,0:T(8,128)} %fusion.23, f32[36,32,8,128]{3,1,2,0:T(8,128)} %copy-done.15, f32[8,128]{1,0:T(8,128)S(1)} %multiply_multiply_fusion.1, f32[32]{0:T(128)S(1)} %copy-done.75, ...), kind=kLoop, calls=%fused_computation.307 | loop fusion | flops 9436160 | bytes 28467328 | tf_op jit(solution)/shard_map/reduce_sum | solution.py:41
  540.7 13.0 %collective-permute-done.32 = f32[36,32,1,128]{3,1,2,0:T(8,128)} collective-permute-done((f32[36,32,1,128]{3,1,2,0:T(8,128)}, f32[36,32,1,128]{3,1,2,0:T(8,128)}, u32[]{:S(2)}, u32[]{:S(2)}) %collective-permute-start.32) | collective-permute-done | bytes 589856 | tf_op jit(solution)/shard_map/ppermute | solution.py:23
  556.9 6.6 %fusion.132 = (f32[36,32,10,1]{3,1,2,0:T(8,128)}, f32[36,32,10,1]{3,1,2,0:T(8,128)}) fusion(f32[36,32,10,128]{3,1,2,0:T(8,128)S(1)} %pad_maximum_fusion.35), kind=kLoop, calls=%fused_computation.310 | loop fusion | bytes 184320 | tf_op jit(solution)/shard_map/slice | solution.py:21
  578.3 8.9 %fusion.25 = f32[36,32,9,128]{3,1,2,0:T(8,128)} fusion(f32[36,32,8,128]{3,1,2,0:T(8,128)} %copy-done.5, f32[36,32,1,128]{3,1,2,0:T(8,128)} %collective-permute-done.32, f32[36,32,1,128]{3,1,2,0:T(8,128)} %collective-permute-done.33, f32[36,32,9,128]{3,1,2,0:T(8,128)} %get-tuple-element.39, f32[9,128]{1,0:T(8,128)S(1)} %copy-done.42), kind=kLoop, calls=%fused_computation.76 | loop fusion | flops 10616832 | bytes 16519680 | tf_op jit(solution)/shard_map/mul | solution.py:55
  593.5 6.3 %copy.251 = f32[36,32,10,1]{3,1,2,0:T(8,128)} copy(f32[36,32,10,1]{0,1,3,2:T(8,128)S(1)} %collective-permute-done.34) | data formatting | bytes 92160 | tf_op jit(solution)/shard_map/ppermute | solution.py:23
  599.8 12.2 %fusion.2 = f32[36,32,8,129]{3,1,2,0:T(8,128)S(1)} fusion(f32[36,32,10,1]{3,1,2,0:T(8,128)} %copy.253, f32[36,32,1,128]{3,1,2,0:T(8,128)} %collective-permute-done.33, f32[36,32,8,128]{3,1,2,0:T(8,128)} %copy-done.5, f32[36,32,1,128]{3,1,2,0:T(8,128)} %collective-permute-done.32, f32[36,32,10,1]{3,1,2,0:T(8,128)} %copy.251, ...), kind=kLoop, calls=%fused_computation.7 | loop fusion | flops 14266368 | bytes 15505440 | tf_op jit(solution)/shard_map/mul | solution.py:61
  617.5 6.5 %copy.257 = f32[36,32,8,128]{3,2,1,0:T(8,128)} copy(f32[36,32,8,128]{3,1,2,0:T(8,128)S(1)} %fusion.34) | data formatting | bytes 9437184
  (408 shorter events, 325.5 us)
Async XLA Ops:
  49.8 39.2 %collective-permute-start = (f32[6,2,128]{2,1,0:T(2,128)}, f32[6,2,128]{2,1,0:T(2,128)S(1)}, u32[]{:S(2)}, u32[]{:S(2)}) collective-permute-start(f32[6,2,128]{2,1,0:T(2,128)} %get-tuple-element.91), channel_id=1, source_target_pairs={{0,2},{2,4},{4,6},{6,8},{8,10},{10,12},{12,14},{14,16},{16,18},{18... | collective-permute-start | bytes 18440 | tf_op jit(solution)/shard_map/ppermute | solution.py:23
  53.5 38.8 %collective-permute-start.1 = (f32[6,2,128]{2,1,0:T(2,128)}, f32[6,2,128]{2,1,0:T(2,128)}, u32[]{:S(2)}, u32[]{:S(2)}) collective-permute-start(f32[6,2,128]{2,1,0:T(2,128)} %get-tuple-element.92), channel_id=1, source_target_pairs={{2,0},{4,2},{6,4},{8,6},{10,8},{12,10},{14,12},{16,14},{18,16},{20... | collective-permute-start | bytes 18440 | tf_op jit(solution)/shard_map/ppermute | solution.py:24
  67.6 163.7 %collective-permute-start.21 = (f32[36,32,1,128]{3,1,2,0:T(8,128)}, f32[36,32,1,128]{3,1,2,0:T(8,128)}, u32[]{:S(2)}, u32[]{:S(2)}) collective-permute-start(f32[36,32,1,128]{3,1,2,0:T(8,128)} %get-tuple-element.71), channel_id=1, source_target_pairs={{2,0},{4,2},{6,4},{8,6},{10,8},{12,10},{14,12},{16,14},{18,16},{20... | collective-permute-start | bytes 1769480 | tf_op jit(solution)/shard_map/ppermute | solution.py:24
  71.8 159.5 %collective-permute-start.20 = (f32[36,32,1,128]{3,1,2,0:T(8,128)}, f32[36,32,1,128]{3,1,2,0:T(8,128)}, u32[]{:S(2)}, u32[]{:S(2)}) collective-permute-start(f32[36,32,1,128]{3,1,2,0:T(8,128)} %get-tuple-element.70), channel_id=1, source_target_pairs={{0,2},{2,4},{4,6},{6,8},{8,10},{10,12},{12,14},{14,16},{16,18},{18... | collective-permute-start | bytes 1769480 | tf_op jit(solution)/shard_map/ppermute | solution.py:23
  75.0 27.8 %collective-permute-start.17 = (f32[6,2,128]{2,1,0:T(2,128)}, f32[6,2,128]{2,1,0:T(2,128)}, u32[]{:S(2)}, u32[]{:S(2)}) collective-permute-start(f32[6,2,128]{2,1,0:T(2,128)} %get-tuple-element.118), channel_id=1, source_target_pairs={{2,0},{4,2},{6,4},{8,6},{10,8},{12,10},{14,12},{16,14},{18,16},{20... | collective-permute-start | bytes 18440 | tf_op jit(solution)/shard_map/ppermute | solution.py:24
  88.9 13.8 %collective-permute-start.16 = (f32[6,2,128]{2,1,0:T(2,128)}, f32[6,2,128]{2,1,0:T(2,128)}, u32[]{:S(2)}, u32[]{:S(2)}) collective-permute-start(f32[6,2,128]{2,1,0:T(2,128)} %get-tuple-element.117), channel_id=1, source_target_pairs={{0,2},{2,4},{4,6},{6,8},{8,10},{10,12},{12,14},{14,16},{16,18},{18... | collective-permute-start | bytes 18440 | tf_op jit(solution)/shard_map/ppermute | solution.py:23
  101.5 22.8 %collective-permute-start.2 = (f32[6,36,2]{1,2,0:T(2,128)}, f32[6,36,2]{1,2,0:T(2,128)S(1)}, u32[]{:S(2)}, u32[]{:S(2)}) collective-permute-start(f32[6,36,2]{1,2,0:T(2,128)} %get-tuple-element.79), channel_id=1, source_target_pairs={{0,1},{2,3},{4,5},{6,7},{8,9},{10,11},{12,13},{14,15},{16,17},{18,... | collective-permute-start | bytes 5192 | tf_op jit(solution)/shard_map/ppermute | solution.py:23
  103.6 6.1 collective-permute-start.19
  104.9 6.3 %collective-permute-start.18 = (f32[6,12,2]{2,1,0:T(8,128)S(1)}, f32[6,12,2]{2,1,0:T(8,128)S(1)}, u32[]{:S(2)}, u32[]{:S(2)}) collective-permute-start(f32[6,12,2]{2,1,0:T(8,128)S(1)} %get-tuple-element.105), channel_id=1, source_target_pairs={{0,1},{2,3},{4,5},{6,7},{8,9},{10,11},{12,13},{14,15},{16,17},{18,... | collective-permute-start | bytes 1736 | tf_op jit(solution)/shard_map/ppermute | solution.py:23
  109.7 14.6 %collective-permute-start.3 = (f32[6,36,2]{1,2,0:T(2,128)}, f32[6,36,2]{1,2,0:T(2,128)S(1)}, u32[]{:S(2)}, u32[]{:S(2)}) collective-permute-start(f32[6,36,2]{1,2,0:T(2,128)} %get-tuple-element.78), channel_id=1, source_target_pairs={{1,0},{3,2},{5,4},{7,6},{9,8},{11,10},{13,12},{15,14},{17,16},{19,... | collective-permute-start | bytes 5192 | tf_op jit(solution)/shard_map/ppermute | solution.py:24
  142.2 17.2 %collective-permute-start.5 = (f32[3,2,128]{2,1,0:T(2,128)S(1)}, f32[3,2,128]{2,1,0:T(2,128)S(1)}, u32[]{:S(2)}, u32[]{:S(2)}) collective-permute-start(f32[3,2,128]{2,1,0:T(2,128)S(1)} %get-tuple-element.112), channel_id=1, source_target_pairs={{2,0},{4,2},{6,4},{8,6},{10,8},{12,10},{14,12},{16,14},{18,16},{20... | collective-permute-start | bytes 9224 | tf_op jit(solution)/shard_map/ppermute | solution.py:24
  144.7 14.8 %collective-permute-start.4 = (f32[3,2,128]{2,1,0:T(2,128)S(1)}, f32[3,2,128]{2,1,0:T(2,128)S(1)}, u32[]{:S(2)}, u32[]{:S(2)}) collective-permute-start(f32[3,2,128]{2,1,0:T(2,128)S(1)} %get-tuple-element.111), channel_id=1, source_target_pairs={{0,2},{2,4},{4,6},{6,8},{8,10},{10,12},{12,14},{14,16},{16,18},{18... | collective-permute-start | bytes 9224 | tf_op jit(solution)/shard_map/ppermute | solution.py:23
  183.0 17.3 %collective-permute-start.9 = (f32[3,2,128]{2,1,0:T(2,128)S(1)}, f32[3,2,128]{2,1,0:T(2,128)S(1)}, u32[]{:S(2)}, u32[]{:S(2)}) collective-permute-start(f32[3,2,128]{2,1,0:T(2,128)S(1)} %get-tuple-element.110), channel_id=1, source_target_pairs={{2,0},{4,2},{6,4},{8,6},{10,8},{12,10},{14,12},{16,14},{18,16},{20... | collective-permute-start | bytes 9224 | tf_op jit(solution)/shard_map/ppermute | solution.py:24
  186.2 14.1 %collective-permute-start.8 = (f32[3,2,128]{2,1,0:T(2,128)S(1)}, f32[3,2,128]{2,1,0:T(2,128)S(1)}, u32[]{:S(2)}, u32[]{:S(2)}) collective-permute-start(f32[3,2,128]{2,1,0:T(2,128)S(1)} %get-tuple-element.109), channel_id=1, source_target_pairs={{0,2},{2,4},{4,6},{6,8},{8,10},{10,12},{12,14},{14,16},{16,18},{18... | collective-permute-start | bytes 9224 | tf_op jit(solution)/shard_map/ppermute | solution.py:23
  224.4 101.7 %collective-permute-start.13 = (f32[3,2,128]{2,1,0:T(2,128)S(1)}, f32[3,2,128]{2,1,0:T(2,128)S(1)}, u32[]{:S(2)}, u32[]{:S(2)}) collective-permute-start(f32[3,2,128]{2,1,0:T(2,128)S(1)} %get-tuple-element.108), channel_id=1, source_target_pairs={{2,0},{4,2},{6,4},{8,6},{10,8},{12,10},{14,12},{16,14},{18,16},{20... | collective-permute-start | bytes 9224 | tf_op jit(solution)/shard_map/ppermute | solution.py:24
  228.5 98.2 %collective-permute-start.12 = (f32[3,2,128]{2,1,0:T(2,128)S(1)}, f32[3,2,128]{2,1,0:T(2,128)}, u32[]{:S(2)}, u32[]{:S(2)}) collective-permute-start(f32[3,2,128]{2,1,0:T(2,128)S(1)} %get-tuple-element.107), channel_id=1, source_target_pairs={{0,2},{2,4},{4,6},{6,8},{8,10},{10,12},{12,14},{14,16},{16,18},{18... | collective-permute-start | bytes 9224 | tf_op jit(solution)/shard_map/ppermute | solution.py:23
  246.3 25.5 %collective-permute-start.23 = (f32[36,32,10,1]{0,1,3,2:T(8,128)S(1)}, f32[36,32,10,1]{0,1,3,2:T(8,128)S(1)}, u32[]{:S(2)}, u32[]{:S(2)}) collective-permute-start(f32[36,32,10,1]{0,1,3,2:T(8,128)S(1)} %copy.240), channel_id=1, source_target_pairs={{1,0},{3,2},{5,4},{7,6},{9,8},{11,10},{13,12},{15,14},{17,16},{19,... | collective-permute-start | bytes 138248 | tf_op jit(solution)/shard_map/ppermute | solution.py:24
  252.7 25.4 %collective-permute-start.22 = (f32[36,32,10,1]{0,1,3,2:T(8,128)S(1)}, f32[36,32,10,1]{0,1,3,2:T(8,128)S(1)}, u32[]{:S(2)}, u32[]{:S(2)}) collective-permute-start(f32[36,32,10,1]{0,1,3,2:T(8,128)S(1)} %copy.238), channel_id=1, source_target_pairs={{0,1},{2,3},{4,5},{6,7},{8,9},{10,11},{12,13},{14,15},{16,17},{18,... | collective-permute-start | bytes 138248 | tf_op jit(solution)/shard_map/ppermute | solution.py:23
  314.1 20.2 %collective-permute-start.25 = (f32[36,32,1,128]{3,1,2,0:T(8,128)}, f32[36,32,1,128]{3,1,2,0:T(8,128)}, u32[]{:S(2)}, u32[]{:S(2)}) collective-permute-start(f32[36,32,1,128]{3,1,2,0:T(8,128)} %get-tuple-element.69), channel_id=1, source_target_pairs={{2,0},{4,2},{6,4},{8,6},{10,8},{12,10},{14,12},{16,14},{18,16},{20... | collective-permute-start | bytes 1769480 | tf_op jit(solution)/shard_map/ppermute | solution.py:24
  318.9 31.2 %collective-permute-start.24 = (f32[36,32,1,128]{3,1,2,0:T(8,128)}, f32[36,32,1,128]{3,1,2,0:T(8,128)}, u32[]{:S(2)}, u32[]{:S(2)}) collective-permute-start(f32[36,32,1,128]{3,1,2,0:T(8,128)} %get-tuple-element.68), channel_id=1, source_target_pairs={{0,2},{2,4},{4,6},{6,8},{8,10},{10,12},{12,14},{14,16},{16,18},{18... | collective-permute-start | bytes 1769480 | tf_op jit(solution)/shard_map/ppermute | solution.py:23
  329.0 100.8 %collective-permute-start.15 = (f32[3,36,2]{1,2,0:T(2,128)S(1)}, f32[3,36,2]{1,2,0:T(2,128)S(1)}, u32[]{:S(2)}, u32[]{:S(2)}) collective-permute-start(f32[3,36,2]{1,2,0:T(2,128)S(1)} %get-tuple-element.81), channel_id=1, source_target_pairs={{1,0},{3,2},{5,4},{7,6},{9,8},{11,10},{13,12},{15,14},{17,16},{19,... | collective-permute-start | bytes 2600 | tf_op jit(solution)/shard_map/ppermute | solution.py:24
  330.3 99.5 %collective-permute-start.14 = (f32[3,36,2]{1,2,0:T(2,128)S(1)}, f32[3,36,2]{1,2,0:T(2,128)S(1)}, u32[]{:S(2)}, u32[]{:S(2)}) collective-permute-start(f32[3,36,2]{1,2,0:T(2,128)S(1)} %get-tuple-element.80), channel_id=1, source_target_pairs={{0,1},{2,3},{4,5},{6,7},{8,9},{10,11},{12,13},{14,15},{16,17},{18,... | collective-permute-start | bytes 2600 | tf_op jit(solution)/shard_map/ppermute | solution.py:23
  365.6 20.3 %collective-permute-start.27 = (f32[36,32,10,1]{0,1,3,2:T(8,128)}, f32[36,32,10,1]{0,1,3,2:T(8,128)}, u32[]{:S(2)}, u32[]{:S(2)}) collective-permute-start(f32[36,32,10,1]{0,1,3,2:T(8,128)} %copy.244), channel_id=1, source_target_pairs={{1,0},{3,2},{5,4},{7,6},{9,8},{11,10},{13,12},{15,14},{17,16},{19,... | collective-permute-start | bytes 138248 | tf_op jit(solution)/shard_map/ppermute | solution.py:24
  372.7 20.4 %collective-permute-start.26 = (f32[36,32,10,1]{0,1,3,2:T(8,128)}, f32[36,32,10,1]{0,1,3,2:T(8,128)}, u32[]{:S(2)}, u32[]{:S(2)}) collective-permute-start(f32[36,32,10,1]{0,1,3,2:T(8,128)} %copy.242), channel_id=1, source_target_pairs={{0,1},{2,3},{4,5},{6,7},{8,9},{10,11},{12,13},{14,15},{16,17},{18,... | collective-permute-start | bytes 138248 | tf_op jit(solution)/shard_map/ppermute | solution.py:23
  421.1 19.1 %collective-permute-start.29 = (f32[36,32,1,128]{3,1,2,0:T(8,128)S(1)}, f32[36,32,1,128]{3,1,2,0:T(8,128)S(1)}, u32[]{:S(2)}, u32[]{:S(2)}) collective-permute-start(f32[36,32,1,128]{3,1,2,0:T(8,128)S(1)} %get-tuple-element.67), channel_id=1, source_target_pairs={{2,0},{4,2},{6,4},{8,6},{10,8},{12,10},{14,12},{16,14},{18,16},{20... | collective-permute-start | bytes 1769480 | tf_op jit(solution)/shard_map/ppermute | solution.py:24
  423.0 24.4 %collective-permute-start.28 = (f32[36,32,1,128]{3,1,2,0:T(8,128)S(1)}, f32[36,32,1,128]{3,1,2,0:T(8,128)S(1)}, u32[]{:S(2)}, u32[]{:S(2)}) collective-permute-start(f32[36,32,1,128]{3,1,2,0:T(8,128)S(1)} %get-tuple-element.66), channel_id=1, source_target_pairs={{0,2},{2,4},{4,6},{6,8},{8,10},{10,12},{12,14},{14,16},{16,18},{18... | collective-permute-start | bytes 1769480 | tf_op jit(solution)/shard_map/ppermute | solution.py:23
  461.2 20.4 %collective-permute-start.31 = (f32[36,32,10,1]{0,1,3,2:T(8,128)}, f32[36,32,10,1]{0,1,3,2:T(8,128)}, u32[]{:S(2)}, u32[]{:S(2)}) collective-permute-start(f32[36,32,10,1]{0,1,3,2:T(8,128)} %copy.248), channel_id=1, source_target_pairs={{1,0},{3,2},{5,4},{7,6},{9,8},{11,10},{13,12},{15,14},{17,16},{19,... | collective-permute-start | bytes 138248 | tf_op jit(solution)/shard_map/ppermute | solution.py:24
  468.2 20.6 %collective-permute-start.30 = (f32[36,32,10,1]{0,1,3,2:T(8,128)}, f32[36,32,10,1]{0,1,3,2:T(8,128)}, u32[]{:S(2)}, u32[]{:S(2)}) collective-permute-start(f32[36,32,10,1]{0,1,3,2:T(8,128)} %copy.246), channel_id=1, source_target_pairs={{0,1},{2,3},{4,5},{6,7},{8,9},{10,11},{12,13},{14,15},{16,17},{18,... | collective-permute-start | bytes 138248 | tf_op jit(solution)/shard_map/ppermute | solution.py:23
  520.6 20.1 %collective-permute-start.33 = (f32[36,32,1,128]{3,1,2,0:T(8,128)}, f32[36,32,1,128]{3,1,2,0:T(8,128)}, u32[]{:S(2)}, u32[]{:S(2)}) collective-permute-start(f32[36,32,1,128]{3,1,2,0:T(8,128)} %get-tuple-element.65), channel_id=1, source_target_pairs={{2,0},{4,2},{6,4},{8,6},{10,8},{12,10},{14,12},{16,14},{18,16},{20... | collective-permute-start | bytes 1769480 | tf_op jit(solution)/shard_map/ppermute | solution.py:24
  522.8 30.9 %collective-permute-start.32 = (f32[36,32,1,128]{3,1,2,0:T(8,128)}, f32[36,32,1,128]{3,1,2,0:T(8,128)}, u32[]{:S(2)}, u32[]{:S(2)}) collective-permute-start(f32[36,32,1,128]{3,1,2,0:T(8,128)} %get-tuple-element.64), channel_id=1, source_target_pairs={{0,2},{2,4},{4,6},{6,8},{8,10},{10,12},{12,14},{14,16},{16,18},{18... | collective-permute-start | bytes 1769480 | tf_op jit(solution)/shard_map/ppermute | solution.py:23
  568.6 18.6 %collective-permute-start.35 = (f32[36,32,10,1]{0,1,3,2:T(8,128)S(1)}, f32[36,32,10,1]{0,1,3,2:T(8,128)S(1)}, u32[]{:S(2)}, u32[]{:S(2)}) collective-permute-start(f32[36,32,10,1]{0,1,3,2:T(8,128)S(1)} %copy.252), channel_id=1, source_target_pairs={{1,0},{3,2},{5,4},{7,6},{9,8},{11,10},{13,12},{15,14},{17,16},{19,... | collective-permute-start | bytes 138248 | tf_op jit(solution)/shard_map/ppermute | solution.py:24
  574.9 18.6 %collective-permute-start.34 = (f32[36,32,10,1]{0,1,3,2:T(8,128)S(1)}, f32[36,32,10,1]{0,1,3,2:T(8,128)S(1)}, u32[]{:S(2)}, u32[]{:S(2)}) collective-permute-start(f32[36,32,10,1]{0,1,3,2:T(8,128)S(1)} %copy.250), channel_id=1, source_target_pairs={{0,1},{2,3},{4,5},{6,7},{8,9},{10,11},{12,13},{14,15},{16,17},{18,... | collective-permute-start | bytes 138248 | tf_op jit(solution)/shard_map/ppermute | solution.py:23
  (104 other events, 1047.2 us)

commit v2 on v1

--- a/solution.py
+++ b/solution.py
@@ -13,82 +13,11 @@
 OSTEPS = 4
 
 
-def padded_2(value, sides, width):
-    for axis, dim in sides:
-        count, length = (lax.axis_size(axis), value.shape[dim])
-        up = [(i, (i + 1) % count) for i in range(count - 1)]
-        down = [(j, i) for i, j in up]
-        last = lax.slice_in_dim(value, length - width, length, axis=dim)
-        initial = lax.slice_in_dim(value, 0, width, axis=dim)
-        before = lax.ppermute(last, axis, up)
-        after = lax.ppermute(initial, axis, down)
-        value = jnp.concatenate([before, value, after], axis=dim)
-    return value
-
-
 def spectral_tables():
     angles = (jnp.arange(ND, dtype=jnp.float32) + 0.5) * (2.0 * math.pi / ND)
     group_speed = 0.5 * jnp.power(jnp.float32(1.1), -jnp.arange(NF, dtype=jnp.float32))
     freq_weight = 2.0 * (jnp.arange(NF, dtype=jnp.float32) + 1.0) / NF
     return (jnp.cos(angles), jnp.sin(angles), group_speed, freq_weight)
-
-
-def source_term(energy, fields, tables):
-    cos_dir, sin_dir, group_speed, freq_weight = tables
-    downwind = jnp.maximum(
-        fields[3][None] * cos_dir[:, None, None] + fields[4][None] * sin_dir[:, None, None], 0.0
-    )
-    column_mean = jnp.mean(energy, axis=(0, 1))
-    damping = 0.3 * jnp.exp(-0.5 * fields[5]) * column_mean
-    growth = 0.02 * downwind[:, None] * freq_weight[None, :, None, None] - damping[None, None]
-    return energy * jnp.exp(growth)
-
-
-def advect(padded, fields, tables):
-    cos_dir, sin_dir, group_speed, freq_weight = tables
-    drift_x, drift_y, wet_cells = (fields[0], fields[1], fields[2])
-    speed_grid = group_speed[None, :, None, None]
-    velocity_x = speed_grid * cos_dir[:, None, None, None] + drift_x[None, None]
-    velocity_y = speed_grid * sin_dir[:, None, None, None] + drift_y[None, None]
-    face_x = 0.5 * (velocity_x[:, :, :-1, 1:-1] + velocity_x[:, :, 1:, 1:-1])
-    open_x = wet_cells[:-1, 1:-1] * wet_cells[1:, 1:-1]
-    flux_x = (
-        jnp.maximum(face_x, 0.0) * padded[:, :, :-1, 1:-1]
-        + jnp.minimum(face_x, 0.0) * padded[:, :, 1:, 1:-1]
-    ) * open_x
-    face_y = 0.5 * (velocity_y[:, :, 1:-1, :-1] + velocity_y[:, :, 1:-1, 1:])
-    open_y = wet_cells[1:-1, :-1] * wet_cells[1:-1, 1:]
-    flux_y = (
-        jnp.maximum(face_y, 0.0) * padded[:, :, 1:-1, :-1]
-        + jnp.minimum(face_y, 0.0) * padded[:, :, 1:-1, 1:]
-    ) * open_y
-    return (
-        padded[:, :, 1:-1, 1:-1]
-        - (flux_x[:, :, 1:] - flux_x[:, :, :-1])
-        - (flux_y[:, :, :, 1:] - flux_y[:, :, :, :-1])
-    )
-
-
-def radiation_stress(energy, tables):
-    cos_dir, sin_dir = (tables[0], tables[1])
-    moments = jnp.stack([cos_dir * cos_dir, cos_dir * sin_dir, sin_dir * sin_dir]) * (
-        0.5 / (ND * NF)
-    )
-    per_direction = jnp.sum(energy, axis=1)
-    return jnp.einsum("cd,dxy->cxy", moments, per_direction, precision=lax.Precision.HIGHEST)
-
-
-def mixing_tendency(profile, top_force, mixing, thickness):
-    interface_flux = mixing[1:, None, None] * (profile[:-1] - profile[1:])
-    bottom = mixing[0] * profile[-1:]
-    fluxes = jnp.concatenate([top_force[None], interface_flux, bottom], axis=0)
-    return (fluxes[:-1] - fluxes[1:]) / thickness[:, None, None]
-
-
-def centered(extended):
-    slope_x = 0.5 * (extended[..., 1:-1, 2:] - extended[..., 1:-1, :-2])
-    slope_y = 0.5 * (extended[..., 2:, 1:-1] - extended[..., :-2, 1:-1])
-    return (slope_x, slope_y)
 
 
 def split_parts(x):
@@ -293,6 +222,413 @@
     return currents, ocean_stress
 
 
+MESH = pl.DeviceIdType.MESH
+
+
+def enter(t, c, tiles):
+    barrier = pltpu.get_barrier_semaphore()
+    has_up, has_down = t > 0, t < tiles - 1
+
+    @pl.when(has_up)
+    def _():
+        pl.semaphore_signal(barrier, inc=1, device_id={"tile": t - 1}, device_id_type=MESH)
+
+    @pl.when(has_down)
+    def _():
+        pl.semaphore_signal(barrier, inc=1, device_id={"tile": t + 1}, device_id_type=MESH)
+
+    pl.semaphore_signal(barrier, inc=1, device_id={"col": 1 - c}, device_id_type=MESH)
+
+    @pl.when(jnp.logical_and(has_up, has_down))
+    def _():
+        pl.semaphore_wait(barrier, 3)
+
+    @pl.when(jnp.logical_not(jnp.logical_and(has_up, has_down)))
+    def _():
+        pl.semaphore_wait(barrier, 2)
+
+    return has_up, has_down
+
+
+def remote(src, dst, send, recv, **where):
+    return pltpu.make_async_remote_copy(
+        src_ref=src, dst_ref=dst, send_sem=send, recv_sem=recv, device_id=where, device_id_type=MESH
+    )
+
+
+CHUNKS = 4
+UNROLL = 8
+
+
+def wave_kernel(
+    spectra, fields, cosd, sind, speed, freq, out,
+    first, last, packed, before, after, beside, f_up, f_down, f_side,
+    s_first, s_last, s_pack, r_before, r_after, r_beside, s_field, r_field,
+):
+    t, c = lax.axis_index("tile"), lax.axis_index("col")
+    tiles = lax.axis_size("tile")
+    has_up, has_down = enter(t, c, tiles)
+    per_chunk = ND // CHUNKS
+    chunk_rows = per_chunk * NF
+    lane = lax.broadcasted_iota(jnp.int32, (8, 128), 1)
+    sub = lax.broadcasted_iota(jnp.int32, (8, 128), 0)
+    edge = jnp.where(c == 0, 127, 0)
+    is0 = jnp.where(c == 0, 1.0, 0.0)
+    is1 = 1.0 - is0
+
+    def field_copies():
+        return (
+            (has_up, remote(fields, f_down, s_field.at[0], r_field.at[1], tile=t - 1),
+             remote(fields, f_up, s_field.at[0], r_field.at[0], tile=t - 1)),
+            (has_down, remote(fields, f_up, s_field.at[1], r_field.at[0], tile=t + 1),
+             remote(fields, f_down, s_field.at[1], r_field.at[1], tile=t + 1)),
+            (None, remote(fields, f_side, s_field.at[2], r_field.at[2], col=1 - c), None),
+        )
+
+    def edge_copies(n, q):
+        rows = pl.ds(pl.multiple_of(q * chunk_rows, 8), chunk_rows)
+        dirs = pl.ds(q * per_chunk, per_chunk)
+        up = remote(first.at[n, rows], after.at[n, rows], s_first.at[n, q], r_after.at[n, q], tile=t - 1)
+        up_in = remote(first.at[n, rows], before.at[n, rows], s_first.at[n, q], r_before.at[n, q], tile=t - 1)
+        down = remote(last.at[n, rows], before.at[n, rows], s_last.at[n, q], r_before.at[n, q], tile=t + 1)
+        down_in = remote(last.at[n, rows], after.at[n, rows], s_last.at[n, q], r_after.at[n, q], tile=t + 1)
+        side = remote(packed.at[n, dirs], beside.at[n, dirs], s_pack.at[n, q], r_beside.at[n, q], col=1 - c)
+        return (has_up, up, up_in), (has_down, down, down_in), (None, side, None)
+
+    def start_all(copies):
+        for cond, out_copy, in_copy in copies:
+            if cond is None:
+                out_copy.start()
+            else:
+                pl.when(cond)(out_copy.start)
+
+    def wait_all(copies):
+        for cond, out_copy, in_copy in copies:
+            if cond is None:
+                out_copy.wait_send()
+                out_copy.wait_recv()
+            else:
+                pl.when(cond)(out_copy.wait_send)
+                pl.when(cond)(in_copy.wait_recv)
+
+    start_all(field_copies())
+
+    @pl.when(jnp.logical_not(has_up))
+    def _():
+        before[...] = jnp.zeros_like(before)
+        f_up[...] = jnp.zeros_like(f_up)
+
+    @pl.when(jnp.logical_not(has_down))
+    def _():
+        after[...] = jnp.zeros_like(after)
+        f_down[...] = jnp.zeros_like(f_down)
+
+    drift_x, drift_y, wet = fields[0], fields[1], fields[2]
+    wind_x, wind_y, level = fields[3], fields[4], fields[5]
+    calm = 0.3 * jnp.exp(-0.5 * level) * (1.0 / (ND * NF))
+
+    def keep_edges(n, d, base, i, f, value, pack):
+        first[n, pl.ds(base + i, 1), :] = value[0:1, :]
+        last[n, pl.ds(base + i, 1), :] = value[7:8, :]
+        shift = lax.rem(f + 256 - edge, 128)
+        return jnp.where(lane == f, pltpu.roll(value, shift, 1), pack)
+
+    def opening(q, total):
+        def one(dd, total):
+            d = q * per_chunk + dd
+
+            def group(fg, carry):
+                total, pack = carry
+                base = pl.multiple_of(d * NF + fg * UNROLL, UNROLL)
+                for i in range(UNROLL):
+                    value = spectra[base + i] * wet
+                    out[base + i] = value
+                    total = total + value
+                    pack = keep_edges(0, d, base, i, fg * UNROLL + i, value, pack)
+                return total, pack
+
+            total, pack = lax.fori_loop(
+                0, NF // UNROLL, group, (total, jnp.zeros((8, 128), jnp.float32))
+            )
+            packed[0, d] = pack
+            return total
+
+        total = lax.fori_loop(0, per_chunk, one, total)
+        start_all(edge_copies(0, q))
+        return total
+
+    total = lax.fori_loop(0, CHUNKS, opening, jnp.zeros((8, 128), jnp.float32))
+    wait_all(field_copies())
+
+    def row_before(i):
+        return jnp.where(sub == 0, f_up[i][7:8], pltpu.roll(fields[i], 1, 0))
+
+    def row_after(i):
+        return jnp.where(sub == 7, f_down[i][0:1], pltpu.roll(fields[i], 7, 0))
+
+    def lane_before(i):
+        return jnp.where(lane == 0, pltpu.roll(f_side[i], 1, 1) * is1, pltpu.roll(fields[i], 1, 1))
+
+    def lane_after(i):
+        return jnp.where(
+            lane == 127, pltpu.roll(f_side[i], 127, 1) * is0, pltpu.roll(fields[i], 127, 1)
+        )
+
+    faces = []
+    for get, i in ((row_before, 0), (row_after, 0), (lane_before, 1), (lane_after, 1)):
+        door = wet * get(2)
+        faces.append((door, door * 0.5 * (fields[i] + get(i))))
+    low_mask = jnp.logical_and(lane == 0, c == 1)
+    high_mask = jnp.logical_and(lane == 127, c == 0)
+
+    def column(i):
+        return jnp.sum(
+            jnp.where(lane == 127 - edge, f_side[i], 0.0), axis=1, keepdims=True
+        ) + jnp.zeros((8, 128), jnp.float32)
+
+    side_x, side_y, side_level = column(3), column(4), column(5)
+    side_calm = 0.3 * jnp.exp(-0.5 * side_level) * (1.0 / (ND * NF))
+    lane_freq = jnp.where(lane < NF, (lane + 1).astype(jnp.float32) * (2.0 / NF), 0.0)
+    freq_column = (
+        lax.broadcasted_iota(jnp.int32, (NF, 128), 0) + 1
+    ).astype(jnp.float32) * (2.0 / NF)
+    rows_of = (
+        (before, f_up[3][7:8], f_up[4][7:8], 0.3 * jnp.exp(-0.5 * f_up[5][7:8]) * (1.0 / (ND * NF))),
+        (after, f_down[3][0:1], f_down[4][0:1], 0.3 * jnp.exp(-0.5 * f_down[5][0:1]) * (1.0 / (ND * NF))),
+    )
+
+    def step(n, total):
+        def arrive(q, carry):
+            wait_all(edge_copies(n, q))
+            return carry
+
+        lax.fori_loop(0, CHUNKS, arrive, 0)
+
+        def add(d, carry):
+            rows = pl.ds(pl.multiple_of(d * NF, NF), NF)
+            return carry[0] + before[n, rows], carry[1] + after[n, rows], carry[2] + beside[n, d]
+
+        zero = jnp.zeros((NF, 128), jnp.float32)
+        sums = lax.fori_loop(0, ND, add, (zero, zero, jnp.zeros((8, 128), jnp.float32)))
+        fades = [jnp.sum(sums[i], axis=0, keepdims=True) * rows_of[i][3] for i in range(2)]
+        side_fade = jnp.sum(sums[2], axis=1, keepdims=True) * side_calm
+        fade = total * calm
+
+        def one(d, total):
+            cos, sin = cosd[d], sind[d]
+            rows = pl.ds(pl.multiple_of(d * NF, NF), NF)
+            for i in range(2):
+                ref, wx, wy, _ = rows_of[i]
+                push = 0.02 * jnp.maximum(wx * cos + wy * sin, 0.0)
+                ref[n, rows] = ref[n, rows] * jnp.exp(push * freq_column - fades[i])
+            push = 0.02 * jnp.maximum(side_x * cos + side_y * sin, 0.0)
+            side = beside[n, d] * jnp.exp(push * lane_freq - side_fade)
+            push = 0.02 * jnp.maximum(wind_x * cos + wind_y * sin, 0.0)
+
+            def group(fg, carry):
+                total, pack = carry
+                base = pl.multiple_of(d * NF + fg * UNROLL, UNROLL)
+                up8 = before[n, pl.ds(base, UNROLL)]
+                down8 = after[n, pl.ds(base, UNROLL)]
+                for i in range(UNROLL):
+                    f = fg * UNROLL + i
+                    e = out[base + i] * jnp.exp(push * freq[f] - fade)
+                    vx, vy = speed[f] * cos, speed[f] * sin
+                    halo = pltpu.roll(side, lax.rem(edge + 128 - f, 128), 1)
+                    x0 = jnp.where(sub == 0, up8[i : i + 1], pltpu.roll(e, 1, 0))
+                    x1 = jnp.where(sub == 7, down8[i : i + 1], pltpu.roll(e, 7, 0))
+                    y0 = jnp.where(low_mask, halo, pltpu.roll(e, 1, 1))
+                    y1 = jnp.where(high_mask, halo, pltpu.roll(e, 127, 1))
+                    wx0 = vx * faces[0][0] + faces[0][1]
+                    wx1 = vx * faces[1][0] + faces[1][1]
+                    wy0 = vy * faces[2][0] + faces[2][1]
+                    wy1 = vy * faces[3][0] + faces[3][1]
+                    fx1 = jnp.maximum(wx1, 0.0) * e + jnp.minimum(wx1, 0.0) * x1
+                    fx0 = jnp.maximum(wx0, 0.0) * x0 + jnp.minimum(wx0, 0.0) * e
+                    fy1 = jnp.maximum(wy1, 0.0) * e + jnp.minimum(wy1, 0.0) * y1
+                    fy0 = jnp.maximum(wy0, 0.0) * y0 + jnp.minimum(wy0, 0.0) * e
+                    value = e - (fx1 - fx0) - (fy1 - fy0)
+                    out[base + i] = value
+                    total = total + value
+                    pack = keep_edges(n + 1, d, base, i, f, value, pack)
+                return total, pack
+
+            total, pack = lax.fori_loop(
+                0, NF // UNROLL, group, (total, jnp.zeros((8, 128), jnp.float32))
+            )
+            packed[n + 1, d] = pack
+            return total
+
+        def chunk(q, total):
+            total = lax.fori_loop(q * per_chunk, (q + 1) * per_chunk, one, total)
+
+            @pl.when(n < WSTEPS - 1)
+            def _():
+                start_all(edge_copies(n + 1, q))
+
+            return total
+
+        return lax.fori_loop(0, CHUNKS, chunk, jnp.zeros((8, 128), jnp.float32))
+
+    lax.fori_loop(0, WSTEPS, step, total)
+
+
+def wave_steps(spectra, fields, tables):
+    _, _, span_x, span_y = spectra.shape
+    bins = ND * NF
+    smem = pl.BlockSpec(memory_space=pltpu.SMEM)
+    dma = pltpu.SemaphoreType.DMA
+    f32 = jnp.float32
+    sems = [dma((WSTEPS, CHUNKS))] * 6 + [dma((3,))] * 2
+    result = pl.pallas_call(
+        wave_kernel,
+        out_shape=jax.ShapeDtypeStruct((bins, span_x, span_y), f32),
+        in_specs=[VMEM, VMEM, smem, smem, smem, smem],
+        out_specs=VMEM,
+        scratch_shapes=[
+            pltpu.VMEM((WSTEPS + 1, bins, span_y), f32),
+            pltpu.VMEM((WSTEPS + 1, bins, span_y), f32),
+            pltpu.VMEM((WSTEPS + 1, ND, span_x, span_y), f32),
+            pltpu.VMEM((WSTEPS, bins, span_y), f32),
+            pltpu.VMEM((WSTEPS, bins, span_y), f32),
+            pltpu.VMEM((WSTEPS, ND, span_x, span_y), f32),
+            pltpu.VMEM((6, span_x, span_y), f32),
+            pltpu.VMEM((6, span_x, span_y), f32),
+            pltpu.VMEM((6, span_x, span_y), f32),
+        ]
+        + sems,
+        compiler_params=pltpu.CompilerParams(
+            collective_id=1, has_side_effects=True, vmem_limit_bytes=48 * 1024 * 1024
+        ),
+    )(spectra.reshape(bins, span_x, span_y), fields, *tables)
+    return result.reshape(ND, NF, span_x, span_y)
+
+
+def ocean_kernel(
+    zonal, meridional, height, stress, sea_in, coriolis_in, thick, inverse, mixing,
+    out_z, out_m, out_h, plane, other, s_up, s_down, r_up, r_down, s_side, r_side,
+):
+    t, c = lax.axis_index("tile"), lax.axis_index("col")
+    tiles = lax.axis_size("tile")
+    levels, rows, cols = zonal.shape
+    has_up, has_down = enter(t, c, tiles)
+    sea = sea_in[...].astype(jnp.float32)
+    coriolis = coriolis_in[...]
+    own = slice(8, 8 + rows)
+    wide = rows + 16
+    lane = lax.broadcasted_iota(jnp.int32, (wide, cols), 1)
+    line = lax.broadcasted_iota(jnp.int32, (wide, cols), 0)
+    first_row = jnp.where(has_up, 0, 8)
+    end_row = jnp.where(has_down, wide, 8 + rows)
+    inside = jnp.where(jnp.logical_and(line >= first_row, line < end_row), 1.0, 0.0)
+    is0 = jnp.where(c == 0, 1.0, 0.0)
+    is1 = 1.0 - is0
+
+    @pl.when(jnp.logical_not(has_up))
+    def _():
+        plane[:, :, 0:8, :] = jnp.zeros((OSTEPS, 6, 8, cols), jnp.float32)
+
+    @pl.when(jnp.logical_not(has_down))
+    def _():
+        plane[:, :, 8 + rows : wide, :] = jnp.zeros((OSTEPS, 6, 8, cols), jnp.float32)
+
+    def dx(value, beside, left, right):
+        ahead = jnp.where(lane == cols - 1, pltpu.roll(beside, cols - 1, 1) * right, pltpu.roll(value, cols - 1, 1))
+        back = jnp.where(lane == 0, pltpu.roll(beside, 1, 1) * left, pltpu.roll(value, 1, 1))
+        return 0.5 * (ahead - back)
+
+    def dy(value):
+        return 0.5 * (pltpu.roll(value, wide - 1, 0) - pltpu.roll(value, 1, 0))
+
+    zero = jnp.zeros((rows, cols), jnp.float32)
+
+    def load(k, carry):
+        z, m = zonal[k] * sea, meridional[k] * sea
+        out_z[k] = z
+        out_m[k] = m
+        return carry[0] + thick[k] * z, carry[1] + thick[k] * m, carry[2] + thick[k]
+
+    tx, ty, depth = lax.fori_loop(0, levels, load, (zero, zero, zero))
+    now = height[...]
+    force_x = force_y = zero
+    for n in range(OSTEPS):
+        plane[n, 0, own, :] = tx / depth
+        plane[n, 1, own, :] = ty / depth
+        plane[n, 2, own, :] = now
+        count = 6 if n == 0 else 3
+        if n == 0:
+            for i in range(3):
+                plane[n, 3 + i, own, :] = stress[i]
+        part = pl.ds(0, count)
+        top, bottom = pl.ds(8, 8), pl.ds(rows, 8)
+        head, tail = pl.ds(0, 8), pl.ds(8 + rows, 8)
+        up = remote(plane.at[n, part, top], plane.at[n, part, tail], s_up.at[n], r_down.at[n], tile=t - 1)
+        up_in = remote(plane.at[n, part, top], plane.at[n, part, head], s_up.at[n], r_up.at[n], tile=t - 1)
+        down = remote(plane.at[n, part, bottom], plane.at[n, part, head], s_down.at[n], r_up.at[n], tile=t + 1)
+        down_in = remote(plane.at[n, part, bottom], plane.at[n, part, tail], s_down.at[n], r_down.at[n], tile=t + 1)
+        pl.when(has_up)(up.start)
+        pl.when(has_down)(down.start)
+        pl.when(has_up)(up.wait_send)
+        pl.when(has_up)(up_in.wait_recv)
+        pl.when(has_down)(down.wait_send)
+        pl.when(has_down)(down_in.wait_recv)
+        side = remote(plane.at[n, part], other.at[n, part], s_side.at[n], r_side.at[n], col=1 - c)
+        side.start()
+        side.wait_send()
+        side.wait_recv()
+        mine = [plane[n, i] for i in range(count)]
+        near = [other[n, i] for i in range(count)]
+        if n == 0:
+            slope = [dx(mine[3 + i], near[3 + i], is1, is0) for i in range(2)]
+            force_x = (-0.5 * (slope[0] + dy(mine[4])))[own]
+            force_y = (-0.5 * (slope[1] + dy(mine[5])))[own]
+        high = (mine[2] - 0.2 * (dx(mine[0], near[0], is1, is0) + dy(mine[1]))) * inside
+        high_near = (near[2] - 0.2 * (dx(near[0], mine[0], is0, is1) + dy(near[1]))) * inside
+        press_x = (0.2 * dx(high, high_near, is1, is0))[own]
+        press_y = (0.2 * dy(high))[own]
+        now = high[own]
+
+        def level(k, carry):
+            tx, ty, flux_z, flux_m, z, m = carry
+            z_next, m_next = out_z[k + 1], out_m[k + 1]
+            low_z = mixing[k + 1] * (z - z_next)
+            low_m = mixing[k + 1] * (m - m_next)
+            new_z = (z + coriolis * m - press_x + (flux_z - low_z) * inverse[k]) * sea
+            new_m = (m - coriolis * z - press_y + (flux_m - low_m) * inverse[k]) * sea
+            out_z[k] = new_z
+            out_m[k] = new_m
+            return tx + thick[k] * new_z, ty + thick[k] * new_m, low_z, low_m, z_next, m_next
+
+        tx, ty, flux_z, flux_m, z, m = lax.fori_loop(
+            0, levels - 1, level, (zero, zero, force_x, force_y, out_z[0], out_m[0])
+        )
+        k = levels - 1
+        new_z = (z + coriolis * m - press_x + (flux_z - mixing[0] * z) * inverse[k]) * sea
+        new_m = (m - coriolis * z - press_y + (flux_m - mixing[0] * m) * inverse[k]) * sea
+        out_z[k] = new_z
+        out_m[k] = new_m
+        tx, ty = tx + thick[k] * new_z, ty + thick[k] * new_m
+    out_h[...] = now
+
+
+def ocean_steps(zonal, meridional, height, stress, sea, coriolis, thickness, mixing):
+    rows, cols = height.shape
+    smem = pl.BlockSpec(memory_space=pltpu.SMEM)
+    f32 = jnp.float32
+    flow = jax.ShapeDtypeStruct(zonal.shape, f32)
+    return pl.pallas_call(
+        ocean_kernel,
+        out_shape=(flow, flow, jax.ShapeDtypeStruct(height.shape, f32)),
+        in_specs=[VMEM] * 6 + [smem] * 3,
+        out_specs=(VMEM, VMEM, VMEM),
+        scratch_shapes=[pltpu.VMEM((OSTEPS, 6, rows + 16, cols), f32)] * 2
+        + [pltpu.SemaphoreType.DMA((OSTEPS,))] * 6,
+        compiler_params=pltpu.CompilerParams(
+            collective_id=2, has_side_effects=True, vmem_limit_bytes=32 * 1024 * 1024
+        ),
+    )(zonal, meridional, height, stress, sea, coriolis, thickness, 1.0 / thickness, mixing)
+
+
 def body(
     zonal_velocity,
     meridional_velocity,
@@ -309,16 +645,13 @@
     remap_weight,
 ):
     tables = spectral_tables()
-    tile_count = lax.axis_size("tile")
-    col_count = lax.axis_size("col")
-    tile_rows, tile_cols = surface_height.shape
+    rows, cols = surface_height.shape
+    total_rows = rows * lax.axis_size("tile")
     sea_cells = ocean_wet.astype(jnp.float32)
     wet_cells = wave_wet.astype(jnp.float32)
-    zonal_flow = zonal_velocity * sea_cells[None]
-    meridional = meridional_velocity * sea_cells[None]
-    height = surface_height
-    energy = spectra * wet_cells[None, None]
-    surface = jnp.stack([zonal_flow[0], meridional[0], height])
+    surface = jnp.stack(
+        [zonal_velocity[0] * sea_cells, meridional_velocity[0] * sea_cells, surface_height]
+    )
     currents, ocean_stress = remap(
         spectra, wave_wet, surface, remap_source, remap_target, remap_weight
     )
@@ -332,60 +665,16 @@
             currents[2],
         ]
     )
-    wide_fields = padded_2(fields, (("tile", 1), ("col", 2)), 2)
-    inner_fields = wide_fields[:, 1:-1, 1:-1]
-    for section_index in range(WSTEPS):
-        energy = source_term(energy, fields, tables)
-        padded = padded_2(energy, (("tile", 2), ("col", 3)), 1)
-        energy = advect(padded, inner_fields, tables)
-    row_start = lax.axis_index("tile") * tile_rows
-    col_start = lax.axis_index("col") * tile_cols
-    total_rows = tile_rows * tile_count
-    total_cols = tile_cols * col_count
+    energy = wave_steps(spectra, fields, tables)
+    row_start = lax.axis_index("tile") * rows
     coriolis = (
-        0.1 + 0.1 * ((row_start + jnp.arange(tile_rows)).astype(jnp.float32) + 0.5) / total_rows
-    )[:, None]
-    edge_rows = row_start + jnp.arange(-1, tile_rows + 1)
-    edge_cols = col_start + jnp.arange(-1, tile_cols + 1)
-    inside = (
-        ((edge_rows >= 0) & (edge_rows < total_rows))[:, None]
-        & ((edge_cols >= 0) & (edge_cols < total_cols))[None, :]
-    ).astype(jnp.float32)
-    column_depth = jnp.sum(thickness)
-    force_x = jnp.zeros_like(height)
-    force_y = jnp.zeros_like(height)
-    for iteration in range(OSTEPS):
-        transport_x = jnp.sum(thickness[:, None, None] * zonal_flow, axis=0) / column_depth
-        transport_y = jnp.sum(thickness[:, None, None] * meridional, axis=0) / column_depth
-        carried = jnp.stack([transport_x, transport_y, height])
-        if iteration == 0:
-            carried = jnp.concatenate([carried, ocean_stress], axis=0)
-        border = padded_2(carried, (("tile", 1), ("col", 2)), 2)
-        if iteration == 0:
-            slope_x, slope_y = centered(border[3:, 1:-1, 1:-1])
-            force_x = -0.5 * (slope_x[0] + slope_y[1])
-            force_y = -0.5 * (slope_x[1] + slope_y[2])
-        diverge_x = 0.5 * (border[0, 1:-1, 2:] - border[0, 1:-1, :-2])
-        diverge_y = 0.5 * (border[1, 2:, 1:-1] - border[1, :-2, 1:-1])
-        margin_height = (border[2, 1:-1, 1:-1] - 0.2 * (diverge_x + diverge_y)) * inside
-        slope_x, slope_y = centered(margin_height)
-        pressure_x = 0.2 * slope_x
-        pressure_y = 0.2 * slope_y
-        new_zonal = (
-            zonal_flow
-            + coriolis * meridional
-            - pressure_x
-            + mixing_tendency(zonal_flow, force_x, mixing, thickness)
-        ) * sea_cells[None]
-        new_meridional = (
-            meridional
-            - coriolis * zonal_flow
-            - pressure_y
-            + mixing_tendency(meridional, force_y, mixing, thickness)
-        ) * sea_cells[None]
-        zonal_flow, meridional = (new_zonal, new_meridional)
-        height = margin_height[1:-1, 1:-1]
-    return (zonal_flow, meridional, height, energy)
+        0.1 + 0.1 * ((row_start + jnp.arange(rows)).astype(jnp.float32) + 0.5) / total_rows
+    )[:, None] + jnp.zeros((rows, cols), jnp.float32)
+    zonal, meridional, height = ocean_steps(
+        zonal_velocity, meridional_velocity, surface_height, ocean_stress, ocean_wet, coriolis,
+        thickness, mixing,
+    )
+    return (zonal, meridional, height, energy)
 
 
 def solution(mesh):

time: 634 us -> 232 us (0.37)
  other arithmetic: 265 us -> 0.2 us
  Pallas kernels: 16.9 us -> 209 us
  local copies, waits for them, and re-layouts: 189 us -> 17.8 us
  starting transfers between devices: 103 us -> 0 us
  waiting for transfers between devices: 47.7 us -> 0 us
    pallas_call x0 -> x2, Pallas kernels: none -> 192 us  [the longest x1 166 us: wave_steps(): pl.pallas_call(wave_kernel, out_shape=jax.ShapeDtypeStruct((bins, span_x,...]
    mul x40 -> x1, other arithmetic: 154 us -> 0.01 us  [body(): zonal_velocity[0] * sea_cells]
    ppermute x36 -> x0, starting transfers between devices: 103 us -> none  [the longest x18 63.2 us: padded_2(): before = lax.ppermute(last, axis, up)]
    slice x23 -> x2, local copies, waits for them, and re-layouts: 77.1 us -> 1.46 us  [the longest x1 0.74 us: body(): zonal_velocity[0] * sea_cells]
    reduce_sum x9 -> x0, other arithmetic: 59.5 us -> none  [the longest x4 36.4 us: body(): jnp.sum(thickness[:, None, None] * zonal_flow, axis=0) / column_depth]
    ppermute x8 -> x0, local copies, waits for them, and re-layouts: 54 us -> none  [the longest x4 27 us: padded_2(): before = lax.ppermute(last, axis, up)]
    ppermute x36 -> x0, waiting for transfers between devices: 47.7 us -> none  [the longest x18 36 us: padded_2(): before = lax.ppermute(last, axis, up)]
    unnamed x211 -> x40, local copies, waits for them, and re-layouts: 40.5 us -> 13.2 us
  transfers between devices with their start and end apart: 36 -> 0, of which waited for: 6 -> 0; matrix products, arithmetic and copies ran while one was open for 52% -> 0% of each run, Pallas kernels for 0% -> 0%
where the time goes in v2:
time: 232 us; the launch traced here: 228 us
  Pallas kernels  209 us (90%)
  local copies, waits for them, and re-layouts  17.8 us (8%)
    pallas_call x1, Pallas kernels, wave_steps(): pl.pallas_call(wave_kernel, out_shape=jax.ShapeDtypeStruct((bins, span_x,...  166 us
    pallas_call x1, Pallas kernels, ocean_steps(): pl.pallas_call(ocean_kernel, out_shape=(flow, flow, jax.ShapeDtypeStruct(...  26.1 us
    unnamed x40, local copies, waits for them, and re-layouts  13.2 us
    pallas_call x1, Pallas kernels, remap(): pl.pallas_call(swap_kernel, out_shape=shape, in_specs=[VMEM], out_specs=V...  8.93 us

profile of v2, /device:TPU:18, one launch (start us, length us, event | category | flops | bytes accessed | tf_op | source)
XLA Modules:
  0.0 227.9 jit_solution(8534241623320306712)
XLA Ops:
  0.7 0.7 slice.27
  1.4 0.1 copy.32
  1.5 0.7 slice.28
  2.2 0.1 copy.33
  2.3 0.8 copy.22
  3.2 0.8 copy.24
  4.0 0.2 copy.30
  4.2 0.2 reshape.85
  4.4 0.7 reshape.78.refs_3_.refs_1_
  5.2 0.7 reshape.79.refs_4_.refs_2_
  5.9 0.7 reshape.80.refs_5_
  6.7 0.0 copy-start
  6.7 2.3 %copy-done = f32[36,32,8,128]{3,2,1,0:T(8,128)S(1)} copy-done((f32[36,32,8,128]{3,2,1,0:T(8,128)S(1)}, f32[36,32,8,128]{3,2,1,0:T(8,128)}, u32[]{:S(2)}) %copy-start) | copy-done | bytes 4718616
  9.0 0.7 copy-done.9
  9.7 3.4 %shard_map.156.src = f32[8,8,512]{2,1,0:T(8,128)S(1)} custom-call(f32[36,32,8,128]{3,2,1,0:T(8,128)S(1)} %copy-done, s32[8,128]{1,0:T(8,128)S(1)} %copy-done.9, f32[8,8,512]{2,1,0:T(8,128)S(1)} %concatenate.4.refs_2_, s32[8,1,512]{2,1,0:T(1,128)S(1)} %reshape.78.refs_3_.refs_1_, s32[8,1,512]{2,1,0:T(1,128)S(1)} %reshape.79.refs_4_.refs_2_, ...), custom_call_target="tpu_custom_call" | custom-call | tf_op jit(solution)/shard_map/pallas_call | solution.py:188
  13.0 0.0 copy-start.5
  13.1 0.7 copy-done.5
  13.7 8.9 %shard_map.157.refs_0_ = f32[8,8,512]{2,1,0:T(8,128)} custom-call(f32[8,8,512]{2,1,0:T(8,128)} %copy-done.5), custom_call_target="tpu_custom_call" | custom-call | tf_op jit(solution)/shard_map/pallas_call | solution.py:196
  22.7 0.9 copy-done.6
  23.6 4.6 %shard_map.158 = (f32[8,1024]{1,0:T(8,128)S(1)}, f32[8,8,512]{2,1,0:T(8,128)S(1)}) custom-call(f32[8,8,512]{2,1,0:T(8,128)S(1)} %copy-done.6, s32[8,1,512]{2,1,0:T(1,128)S(1)} %reshape.78.refs_3_.refs_1_, s32[8,1,512]{2,1,0:T(1,128)S(1)} %reshape.79.refs_4_.refs_2_), custom_call_target="tpu_custom_call" | custom-call | tf_op jit(solution)/shard_map/pallas_call | solution.py:208
  28.4 0.0 copy-start.4
  28.5 165.9 %shard_map.160 = f32[1152,8,128]{2,1,0:T(8,128)S(1)} custom-call(f32[1152,8,128]{2,1,0:T(8,128)} %bitcast.26, f32[6,8,128]{2,1,0:T(8,128)S(1)} %constant_dynamic-update-slice_fusion.fields, f32[36]{0:T(128)S(1)} %get-tuple-element.22.cosd, f32[36]{0:T(128)S(1)} %get-tuple-element.21.sind, f32[32]{0:T(128)S(1)} %get-tuple-element.20.speed, ...), custom_call_target="tpu_custom_call" | custom-call | tf_op jit(solution)/shard_map/pallas_call | solution.py:483
  194.5 2.2 copy-done.1
  196.7 0.2 reshape.81
  196.8 0.2 copy.28
  197.0 0.1 copy.29.stress
  197.1 0.1 add.49.coriolis_in
  197.3 26.1 %shard_map.159 = (f32[50,32,128]{2,1,0:T(8,128)S(1)}, f32[50,32,128]{2,1,0:T(8,128)S(1)}, f32[32,128]{1,0:T(8,128)S(1)}) custom-call(f32[50,32,128]{2,1,0:T(8,128)S(1)} %copy-done.3, f32[50,32,128]{2,1,0:T(8,128)S(1)} %copy-done.4, f32[32,128]{1,0:T(8,128)S(1)} %copy-done.7, f32[3,32,128]{2,1,0:T(8,128)S(1)} %copy.29.stress, s32[32,128]{1,0:T(8,128)S(1)} %copy-done.8, ...), custom_call_target="tpu_custom_call" | custom-call | tf_op jit(solution)/shard_map/pallas_call | solution.py:619
  223.4 0.9 copy.43
  224.3 0.9 copy.44
  225.1 0.6 copy.45
  225.8 2.2 copy.46
  (38 shorter events, 0.3 us)
Async XLA Ops:
  0.6 27.6 %copy-start.10 = (s32[8,128]{1,0:T(8,128)S(1)}, s32[8,128]{1,0:T(8,128)}, u32[]{:S(2)}) copy-start(s32[8,128]{1,0:T(8,128)} %refs_1_.1) | copy-start | bytes 12292
  0.6 27.6 %copy-start.13 = (f32[8,128]{1,0:T(8,128)S(1)}, f32[8,128]{1,0:T(8,128)}, u32[]{:S(2)}) copy-start(f32[8,128]{1,0:T(8,128)} %param.20) | copy-start | bytes 12292
  0.7 27.6 %copy-start.14 = (f32[8,128]{1,0:T(8,128)S(1)}, f32[8,128]{1,0:T(8,128)}, u32[]{:S(2)}) copy-start(f32[8,128]{1,0:T(8,128)} %param.21) | copy-start | bytes 12292
  6.7 2.3 %copy-start = (f32[36,32,8,128]{3,2,1,0:T(8,128)S(1)}, f32[36,32,8,128]{3,2,1,0:T(8,128)}, u32[]{:S(2)}) copy-start(f32[36,32,8,128]{3,2,1,0:T(8,128)} %refs_0_.1) | copy-start | bytes 14155780
  9.0 0.7 copy-start.9
  13.0 0.7 copy-start.5
  22.6 0.9 copy-start.6
  28.4 168.8 %copy-start.11 = (f32[50]{0:T(128)S(1)}, f32[50]{0:T(128)}, u32[]{:S(2)}) copy-start(f32[50]{0:T(128)} %thick.1) | copy-start | bytes 604
  28.4 168.8 %copy-start.3 = (f32[50,32,128]{2,1,0:T(8,128)S(1)}, f32[50,32,128]{2,1,0:T(8,128)}, u32[]{:S(2)}) copy-start(f32[50,32,128]{2,1,0:T(8,128)} %zonal.1) | copy-start | bytes 2457604
  28.4 168.8 %copy-start.4 = (f32[50,32,128]{2,1,0:T(8,128)S(1)}, f32[50,32,128]{2,1,0:T(8,128)}, u32[]{:S(2)}) copy-start(f32[50,32,128]{2,1,0:T(8,128)} %meridional.1) | copy-start | bytes 2457604
  28.5 168.8 %copy-start.7 = (f32[32,128]{1,0:T(8,128)S(1)}, f32[32,128]{1,0:T(8,128)}, u32[]{:S(2)}) copy-start(f32[32,128]{1,0:T(8,128)} %height.1) | copy-start | bytes 49156
  28.5 168.8 %copy-start.8 = (s32[32,128]{1,0:T(8,128)S(1)}, s32[32,128]{1,0:T(8,128)}, u32[]{:S(2)}) copy-start(s32[32,128]{1,0:T(8,128)} %sea_in.1) | copy-start | bytes 49156
  28.5 168.8 %copy-start.12 = (f32[50]{0:T(128)S(1)}, f32[50]{0:T(128)}, u32[]{:S(2)}) copy-start(f32[50]{0:T(128)} %mixing.1) | copy-start | bytes 604
  194.4 2.2 copy-start.1
  197.1 28.7 %copy-start.2 = (f32[1152,8,128]{2,1,0:T(8,128)S(1)}, f32[1152,8,128]{2,1,0:T(8,128)}, u32[]{:S(2)}) copy-start(f32[1152,8,128]{2,1,0:T(8,128)} %copy-done.1) | copy-start | bytes 14155780

commit v3 on v2

--- a/solution.py
+++ b/solution.py
@@ -257,7 +257,8 @@
 
 
 CHUNKS = 4
-UNROLL = 8
+UNROLL = 32
+LEVELS = 7
 
 
 def wave_kernel(
@@ -599,9 +600,15 @@
             out_m[k] = new_m
             return tx + thick[k] * new_z, ty + thick[k] * new_m, low_z, low_m, z_next, m_next
 
-        tx, ty, flux_z, flux_m, z, m = lax.fori_loop(
-            0, levels - 1, level, (zero, zero, force_x, force_y, out_z[0], out_m[0])
-        )
+        def several(g, carry):
+            for i in range(LEVELS):
+                carry = level(g * LEVELS + i, carry)
+            return carry
+
+        carry = (zero, zero, force_x, force_y, out_z[0], out_m[0])
+        groups = (levels - 1) // LEVELS
+        carry = lax.fori_loop(0, groups, several, carry)
+        tx, ty, flux_z, flux_m, z, m = lax.fori_loop(groups * LEVELS, levels - 1, level, carry)
         k = levels - 1
         new_z = (z + coriolis * m - press_x + (flux_z - mixing[0] * z) * inverse[k]) * sea
         new_m = (m - coriolis * z - press_y + (flux_m - mixing[0] * m) * inverse[k]) * sea

time: 232 us -> 198 us (0.85)
  Pallas kernels: 209 us -> 175 us
    pallas_call x1, Pallas kernels: 166 us -> 133 us  [wave_steps(): pl.pallas_call(wave_kernel, out_shape=jax.ShapeDtypeStruct((bins, span_x,...]
where the time goes in v3:
time: 198 us; the launch traced here: 194 us
  Pallas kernels  175 us (88%)
  local copies, waits for them, and re-layouts  17.8 us (9%)
    pallas_call x1, Pallas kernels, wave_steps(): pl.pallas_call(wave_kernel, out_shape=jax.ShapeDtypeStruct((bins, span_x,...  133 us
    pallas_call x1, Pallas kernels, ocean_steps(): pl.pallas_call(ocean_kernel, out_shape=(flow, flow, jax.ShapeDtypeStruct(...  24.6 us
    unnamed x40, local copies, waits for them, and re-layouts  13.2 us
    pallas_call x1, Pallas kernels, remap(): pl.pallas_call(swap_kernel, out_shape=shape, in_specs=[VMEM], out_specs=V...  8.93 us
    pallas_call x1, Pallas kernels, remap(): pl.pallas_call(lambda *refs: scatter_kernel(cols, width, *refs), out_shap...  4.62 us

profile of v3, /device:TPU:18, one launch (start us, length us, event | category | flops | bytes accessed | tf_op | source)
XLA Modules:
  0.0 194.0 jit_solution(13004330735501346169)
XLA Ops:
  0.7 0.7 slice.27
  1.4 0.1 copy.32
  1.5 0.7 slice.28
  2.2 0.1 copy.33
  2.3 0.8 copy.22
  3.2 0.8 copy.24
  4.0 0.2 copy.30
  4.2 0.2 reshape.85
  4.4 0.7 reshape.78.refs_3_.refs_1_
  5.2 0.7 reshape.79.refs_4_.refs_2_
  5.9 0.7 reshape.80.refs_5_
  6.7 0.0 copy-start
  6.7 2.3 %copy-done = f32[36,32,8,128]{3,2,1,0:T(8,128)S(1)} copy-done((f32[36,32,8,128]{3,2,1,0:T(8,128)S(1)}, f32[36,32,8,128]{3,2,1,0:T(8,128)}, u32[]{:S(2)}) %copy-start) | copy-done | bytes 4718616
  9.0 0.7 copy-done.9
  9.7 3.4 %shard_map.156.src = f32[8,8,512]{2,1,0:T(8,128)S(1)} custom-call(f32[36,32,8,128]{3,2,1,0:T(8,128)S(1)} %copy-done, s32[8,128]{1,0:T(8,128)S(1)} %copy-done.9, f32[8,8,512]{2,1,0:T(8,128)S(1)} %concatenate.4.refs_2_, s32[8,1,512]{2,1,0:T(1,128)S(1)} %reshape.78.refs_3_.refs_1_, s32[8,1,512]{2,1,0:T(1,128)S(1)} %reshape.79.refs_4_.refs_2_, ...), custom_call_target="tpu_custom_call" | custom-call | tf_op jit(solution)/shard_map/pallas_call | solution.py:188
  13.0 0.0 copy-start.5
  13.1 0.7 copy-done.5
  13.7 8.9 %shard_map.157.refs_0_ = f32[8,8,512]{2,1,0:T(8,128)} custom-call(f32[8,8,512]{2,1,0:T(8,128)} %copy-done.5), custom_call_target="tpu_custom_call" | custom-call | tf_op jit(solution)/shard_map/pallas_call | solution.py:196
  22.7 0.9 copy-done.6
  23.6 4.6 %shard_map.158 = (f32[8,1024]{1,0:T(8,128)S(1)}, f32[8,8,512]{2,1,0:T(8,128)S(1)}) custom-call(f32[8,8,512]{2,1,0:T(8,128)S(1)} %copy-done.6, s32[8,1,512]{2,1,0:T(1,128)S(1)} %reshape.78.refs_3_.refs_1_, s32[8,1,512]{2,1,0:T(1,128)S(1)} %reshape.79.refs_4_.refs_2_), custom_call_target="tpu_custom_call" | custom-call | tf_op jit(solution)/shard_map/pallas_call | solution.py:208
  28.4 0.0 copy-start.4
  28.5 133.5 %shard_map.160 = f32[1152,8,128]{2,1,0:T(8,128)S(1)} custom-call(f32[1152,8,128]{2,1,0:T(8,128)} %bitcast.26, f32[6,8,128]{2,1,0:T(8,128)S(1)} %constant_dynamic-update-slice_fusion.fields, f32[36]{0:T(128)S(1)} %get-tuple-element.22.cosd, f32[36]{0:T(128)S(1)} %get-tuple-element.21.sind, f32[32]{0:T(128)S(1)} %get-tuple-element.20.speed, ...), custom_call_target="tpu_custom_call" | custom-call | tf_op jit(solution)/shard_map/pallas_call | solution.py:484
  162.0 2.2 %copy-done.1 = f32[1152,8,128]{2,1,0:T(8,128)} copy-done((f32[1152,8,128]{2,1,0:T(8,128)}, f32[1152,8,128]{2,1,0:T(8,128)S(1)}, u32[]{:S(2)}) %copy-start.1) | copy-done | bytes 4718616
  164.2 0.2 reshape.81
  164.4 0.2 copy.28
  164.5 0.1 copy.29.stress
  164.7 0.1 add.49.coriolis_in
  164.8 24.6 %shard_map.159 = (f32[50,32,128]{2,1,0:T(8,128)S(1)}, f32[50,32,128]{2,1,0:T(8,128)S(1)}, f32[32,128]{1,0:T(8,128)S(1)}) custom-call(f32[50,32,128]{2,1,0:T(8,128)S(1)} %copy-done.3, f32[50,32,128]{2,1,0:T(8,128)S(1)} %copy-done.4, f32[32,128]{1,0:T(8,128)S(1)} %copy-done.7, f32[3,32,128]{2,1,0:T(8,128)S(1)} %copy.29.stress, s32[32,128]{1,0:T(8,128)S(1)} %copy-done.8, ...), custom_call_target="tpu_custom_call" | custom-call | tf_op jit(solution)/shard_map/pallas_call | solution.py:626
  189.4 0.9 copy.43
  190.3 0.9 copy.44
  191.2 0.6 copy.45
  191.8 2.2 %copy.46 = f32[36,32,8,128]{3,2,1,0:T(8,128)} copy(f32[36,32,8,128]{3,2,1,0:T(8,128)S(1)} %bitcast.27) | data formatting | bytes 9437184
  (38 shorter events, 0.3 us)
Async XLA Ops:
  0.6 27.6 %copy-start.10 = (s32[8,128]{1,0:T(8,128)S(1)}, s32[8,128]{1,0:T(8,128)}, u32[]{:S(2)}) copy-start(s32[8,128]{1,0:T(8,128)} %refs_1_.1) | copy-start | bytes 12292
  0.6 27.6 %copy-start.13 = (f32[8,128]{1,0:T(8,128)S(1)}, f32[8,128]{1,0:T(8,128)}, u32[]{:S(2)}) copy-start(f32[8,128]{1,0:T(8,128)} %param.20) | copy-start | bytes 12292
  0.7 27.6 %copy-start.14 = (f32[8,128]{1,0:T(8,128)S(1)}, f32[8,128]{1,0:T(8,128)}, u32[]{:S(2)}) copy-start(f32[8,128]{1,0:T(8,128)} %param.21) | copy-start | bytes 12292
  6.7 2.3 %copy-start = (f32[36,32,8,128]{3,2,1,0:T(8,128)S(1)}, f32[36,32,8,128]{3,2,1,0:T(8,128)}, u32[]{:S(2)}) copy-start(f32[36,32,8,128]{3,2,1,0:T(8,128)} %refs_0_.1) | copy-start | bytes 14155780
  9.0 0.7 copy-start.9
  13.0 0.7 copy-start.5
  22.6 0.9 copy-start.6
  28.4 136.3 %copy-start.11 = (f32[50]{0:T(128)S(1)}, f32[50]{0:T(128)}, u32[]{:S(2)}) copy-start(f32[50]{0:T(128)} %thick.1) | copy-start | bytes 604
  28.4 136.3 %copy-start.3 = (f32[50,32,128]{2,1,0:T(8,128)S(1)}, f32[50,32,128]{2,1,0:T(8,128)}, u32[]{:S(2)}) copy-start(f32[50,32,128]{2,1,0:T(8,128)} %zonal.1) | copy-start | bytes 2457604
  28.4 136.3 %copy-start.4 = (f32[50,32,128]{2,1,0:T(8,128)S(1)}, f32[50,32,128]{2,1,0:T(8,128)}, u32[]{:S(2)}) copy-start(f32[50,32,128]{2,1,0:T(8,128)} %meridional.1) | copy-start | bytes 2457604
  28.5 136.3 %copy-start.7 = (f32[32,128]{1,0:T(8,128)S(1)}, f32[32,128]{1,0:T(8,128)}, u32[]{:S(2)}) copy-start(f32[32,128]{1,0:T(8,128)} %height.1) | copy-start | bytes 49156
  28.5 136.3 %copy-start.8 = (s32[32,128]{1,0:T(8,128)S(1)}, s32[32,128]{1,0:T(8,128)}, u32[]{:S(2)}) copy-start(s32[32,128]{1,0:T(8,128)} %sea_in.1) | copy-start | bytes 49156
  28.5 136.3 %copy-start.12 = (f32[50]{0:T(128)S(1)}, f32[50]{0:T(128)}, u32[]{:S(2)}) copy-start(f32[50]{0:T(128)} %mixing.1) | copy-start | bytes 604
  162.0 2.2 %copy-start.1 = (f32[1152,8,128]{2,1,0:T(8,128)}, f32[1152,8,128]{2,1,0:T(8,128)S(1)}, u32[]{:S(2)}) copy-start(f32[1152,8,128]{2,1,0:T(8,128)S(1)} %shard_map.160) | copy-start | bytes 14155780
  164.6 27.1 %copy-start.2 = (f32[1152,8,128]{2,1,0:T(8,128)S(1)}, f32[1152,8,128]{2,1,0:T(8,128)}, u32[]{:S(2)}) copy-start(f32[1152,8,128]{2,1,0:T(8,128)} %copy-done.1) | copy-start | bytes 14155780

commit v4 on v3

--- a/solution.py
+++ b/solution.py
@@ -262,7 +262,7 @@
 
 
 def wave_kernel(
-    spectra, fields, cosd, sind, speed, freq, out,
+    beside_work, spectra, fields, cosd, sind, speed, freq, out,
     first, last, packed, before, after, beside, f_up, f_down, f_side,
     s_first, s_last, s_pack, r_before, r_after, r_beside, s_field, r_field,
 ):
@@ -359,6 +359,7 @@
         return total
 
     total = lax.fori_loop(0, CHUNKS, opening, jnp.zeros((8, 128), jnp.float32))
+    beside_work()
     wait_all(field_copies())
 
     def row_before(i):
@@ -474,37 +475,6 @@
     lax.fori_loop(0, WSTEPS, step, total)
 
 
-def wave_steps(spectra, fields, tables):
-    _, _, span_x, span_y = spectra.shape
-    bins = ND * NF
-    smem = pl.BlockSpec(memory_space=pltpu.SMEM)
-    dma = pltpu.SemaphoreType.DMA
-    f32 = jnp.float32
-    sems = [dma((WSTEPS, CHUNKS))] * 6 + [dma((3,))] * 2
-    result = pl.pallas_call(
-        wave_kernel,
-        out_shape=jax.ShapeDtypeStruct((bins, span_x, span_y), f32),
-        in_specs=[VMEM, VMEM, smem, smem, smem, smem],
-        out_specs=VMEM,
-        scratch_shapes=[
-            pltpu.VMEM((WSTEPS + 1, bins, span_y), f32),
-            pltpu.VMEM((WSTEPS + 1, bins, span_y), f32),
-            pltpu.VMEM((WSTEPS + 1, ND, span_x, span_y), f32),
-            pltpu.VMEM((WSTEPS, bins, span_y), f32),
-            pltpu.VMEM((WSTEPS, bins, span_y), f32),
-            pltpu.VMEM((WSTEPS, ND, span_x, span_y), f32),
-            pltpu.VMEM((6, span_x, span_y), f32),
-            pltpu.VMEM((6, span_x, span_y), f32),
-            pltpu.VMEM((6, span_x, span_y), f32),
-        ]
-        + sems,
-        compiler_params=pltpu.CompilerParams(
-            collective_id=1, has_side_effects=True, vmem_limit_bytes=48 * 1024 * 1024
-        ),
-    )(spectra.reshape(bins, span_x, span_y), fields, *tables)
-    return result.reshape(ND, NF, span_x, span_y)
-
-
 def ocean_kernel(
     zonal, meridional, height, stress, sea_in, coriolis_in, thick, inverse, mixing,
     out_z, out_m, out_h, plane, other, s_up, s_down, r_up, r_down, s_side, r_side,
@@ -512,7 +482,7 @@
     t, c = lax.axis_index("tile"), lax.axis_index("col")
     tiles = lax.axis_size("tile")
     levels, rows, cols = zonal.shape
-    has_up, has_down = enter(t, c, tiles)
+    has_up, has_down = t > 0, t < tiles - 1
     sea = sea_in[...].astype(jnp.float32)
     coriolis = coriolis_in[...]
     own = slice(8, 8 + rows)
@@ -618,22 +588,57 @@
     out_h[...] = now
 
 
-def ocean_steps(zonal, meridional, height, stress, sea, coriolis, thickness, mixing):
+def both_kernel(*refs):
+    waves_in, ocean_in, wave_out, ocean_out = refs[:6], refs[6:15], refs[15], refs[16:19]
+    waves_scratch, ocean_scratch = refs[19:36], refs[36:]
+
+    def ocean():
+        ocean_kernel(*ocean_in, *ocean_out, *ocean_scratch)
+
+    wave_kernel(ocean, *waves_in, wave_out, *waves_scratch)
+
+
+def both_steps(spectra, fields, tables, zonal, meridional, height, stress, sea, coriolis, thickness, mixing):
+    _, _, span_x, span_y = spectra.shape
     rows, cols = height.shape
+    bins = ND * NF
     smem = pl.BlockSpec(memory_space=pltpu.SMEM)
+    dma = pltpu.SemaphoreType.DMA
     f32 = jnp.float32
     flow = jax.ShapeDtypeStruct(zonal.shape, f32)
-    return pl.pallas_call(
-        ocean_kernel,
-        out_shape=(flow, flow, jax.ShapeDtypeStruct(height.shape, f32)),
-        in_specs=[VMEM] * 6 + [smem] * 3,
-        out_specs=(VMEM, VMEM, VMEM),
-        scratch_shapes=[pltpu.VMEM((OSTEPS, 6, rows + 16, cols), f32)] * 2
-        + [pltpu.SemaphoreType.DMA((OSTEPS,))] * 6,
+    energy, new_zonal, new_meridional, new_height = pl.pallas_call(
+        both_kernel,
+        out_shape=(
+            jax.ShapeDtypeStruct((bins, span_x, span_y), f32),
+            flow,
+            flow,
+            jax.ShapeDtypeStruct(height.shape, f32),
+        ),
+        in_specs=[VMEM] * 2 + [smem] * 4 + [VMEM] * 6 + [smem] * 3,
+        out_specs=(VMEM, VMEM, VMEM, VMEM),
+        scratch_shapes=[
+            pltpu.VMEM((WSTEPS + 1, bins, span_y), f32),
+            pltpu.VMEM((WSTEPS + 1, bins, span_y), f32),
+            pltpu.VMEM((WSTEPS + 1, ND, span_x, span_y), f32),
+            pltpu.VMEM((WSTEPS, bins, span_y), f32),
+            pltpu.VMEM((WSTEPS, bins, span_y), f32),
+            pltpu.VMEM((WSTEPS, ND, span_x, span_y), f32),
+            pltpu.VMEM((6, span_x, span_y), f32),
+            pltpu.VMEM((6, span_x, span_y), f32),
+            pltpu.VMEM((6, span_x, span_y), f32),
+        ]
+        + [dma((WSTEPS, CHUNKS))] * 6
+        + [dma((3,))] * 2
+        + [pltpu.VMEM((OSTEPS, 6, rows + 16, cols), f32)] * 2
+        + [dma((OSTEPS,))] * 6,
         compiler_params=pltpu.CompilerParams(
-            collective_id=2, has_side_effects=True, vmem_limit_bytes=32 * 1024 * 1024
+            collective_id=1, has_side_effects=True, vmem_limit_bytes=48 * 1024 * 1024
         ),
-    )(zonal, meridional, height, stress, sea, coriolis, thickness, 1.0 / thickness, mixing)
+    )(
+        spectra.reshape(bins, span_x, span_y), fields, *tables,
+        zonal, meridional, height, stress, sea, coriolis, thickness, 1.0 / thickness, mixing,
+    )
+    return new_zonal, new_meridional, new_height, energy.reshape(spectra.shape)
 
 
 def body(
@@ -672,16 +677,14 @@
             currents[2],
         ]
     )
-    energy = wave_steps(spectra, fields, tables)
     row_start = lax.axis_index("tile") * rows
     coriolis = (
         0.1 + 0.1 * ((row_start + jnp.arange(rows)).astype(jnp.float32) + 0.5) / total_rows
     )[:, None] + jnp.zeros((rows, cols), jnp.float32)
-    zonal, meridional, height = ocean_steps(
-        zonal_velocity, meridional_velocity, surface_height, ocean_stress, ocean_wet, coriolis,
+    return both_steps(
+        spectra, fields, tables, zonal_velocity, meridional_velocity, surface_height, ocean_stress, ocean_wet, coriolis,
         thickness, mixing,
     )
-    return (zonal, meridional, height, energy)
 
 
 def solution(mesh):

time: 198 us -> 196 us (0.990)
  Pallas kernels: 175 us -> 173 us
    pallas_call x2 -> x1, Pallas kernels: 158 us -> 156 us  [both_steps(): pl.pallas_call(both_kernel, out_shape=(jax.ShapeDtypeStruct((bins, span_x...]
    unnamed x40 -> x36, local copies, waits for them, and re-layouts: 13.2 us -> 13.9 us
where the time goes in v4:
time: 196 us; the launch traced here: 193 us
  Pallas kernels  173 us (88%)
  local copies, waits for them, and re-layouts  18.6 us (9%)
    pallas_call x1, Pallas kernels, both_steps(): pl.pallas_call(both_kernel, out_shape=(jax.ShapeDtypeStruct((bins, span_x...  156 us
    unnamed x36, local copies, waits for them, and re-layouts  13.9 us
    pallas_call x1, Pallas kernels, remap(): pl.pallas_call(swap_kernel, out_shape=shape, in_specs=[VMEM], out_specs=V...  8.95 us
    pallas_call x1, Pallas kernels, remap(): pl.pallas_call(lambda *refs: scatter_kernel(cols, width, *refs), out_shap...  4.62 us

profile of v4, /device:TPU:18, one launch (start us, length us, event | category | flops | bytes accessed | tf_op | source)
XLA Modules:
  0.0 193.4 jit_solution(3987390147879736417)
XLA Ops:
  0.6 0.0 copy-start.8
  0.7 0.7 broadcast_divide_fusion.refs_13_
  1.4 0.1 add.53.refs_11_
  1.5 0.7 reshape.79.refs_3_.refs_1_
  2.2 0.7 reshape.80.refs_4_.refs_2_
  3.0 0.7 reshape.81.refs_5_
  3.7 0.7 slice.27
  4.4 0.0 copy-start.9
  4.4 0.8 slice.28
  5.3 0.1 copy.33
  5.4 0.1 copy.32
  5.5 0.8 copy.24
  6.3 0.8 copy.22
  7.2 0.2 copy.30
  7.4 0.2 reshape.85
  7.6 0.0 copy-start
  7.6 2.3 %copy-done = f32[36,32,8,128]{3,2,1,0:T(8,128)S(1)} copy-done((f32[36,32,8,128]{3,2,1,0:T(8,128)S(1)}, f32[36,32,8,128]{3,2,1,0:T(8,128)}, u32[]{:S(2)}) %copy-start) | copy-done | bytes 4718616
  10.0 0.7 copy-done.7
  10.6 3.4 %shard_map.156.src = f32[8,8,512]{2,1,0:T(8,128)S(1)} custom-call(f32[36,32,8,128]{3,2,1,0:T(8,128)S(1)} %copy-done, s32[8,128]{1,0:T(8,128)S(1)} %copy-done.7, f32[8,8,512]{2,1,0:T(8,128)S(1)} %concatenate.4.refs_2_, s32[8,1,512]{2,1,0:T(1,128)S(1)} %reshape.79.refs_3_.refs_1_, s32[8,1,512]{2,1,0:T(1,128)S(1)} %reshape.80.refs_4_.refs_2_, ...), custom_call_target="tpu_custom_call" | custom-call | tf_op jit(solution)/shard_map/pallas_call | solution.py:188
  14.0 0.0 copy-start.3
  14.0 0.7 copy-done.3
  14.7 9.0 %shard_map.157.refs_0_ = f32[8,8,512]{2,1,0:T(8,128)} custom-call(f32[8,8,512]{2,1,0:T(8,128)} %copy-done.3), custom_call_target="tpu_custom_call" | custom-call | tf_op jit(solution)/shard_map/pallas_call | solution.py:196
  23.6 0.9 copy-done.4
  24.5 4.6 %shard_map.158 = (f32[8,1024]{1,0:T(8,128)S(1)}, f32[8,8,512]{2,1,0:T(8,128)S(1)}) custom-call(f32[8,8,512]{2,1,0:T(8,128)S(1)} %copy-done.4, s32[8,1,512]{2,1,0:T(1,128)S(1)} %reshape.79.refs_3_.refs_1_, s32[8,1,512]{2,1,0:T(1,128)S(1)} %reshape.80.refs_4_.refs_2_), custom_call_target="tpu_custom_call" | custom-call | tf_op jit(solution)/shard_map/pallas_call | solution.py:208
  29.4 0.2 reshape.82
  29.6 0.2 copy.28
  29.7 0.1 copy.29.refs_9_
  29.9 156.1 %shard_map.159 = (f32[1152,8,128]{2,1,0:T(8,128)}, f32[50,32,128]{2,1,0:T(8,128)S(1)}, f32[50,32,128]{2,1,0:T(8,128)S(1)}, f32[32,128]{1,0:T(8,128)S(1)}) custom-call(f32[1152,8,128]{2,1,0:T(8,128)} %bitcast.26, f32[6,8,128]{2,1,0:T(8,128)S(1)} %constant_dynamic-update-slice_fusion.refs_1_, f32[36]{0:T(128)S(1)} %get-tuple-element.24.refs_2_, ...), custom_call_target="tpu_custom_call" | custom-call | tf_op jit(solution)/shard_map/pallas_call | solution.py:609
  186.0 0.9 copy.43
  186.9 0.9 copy.44
  187.8 0.6 copy.45
  188.4 5.0 %copy.46 = f32[36,32,8,128]{3,2,1,0:T(8,128)} copy(f32[36,32,8,128]{3,2,1,0:T(8,128)} %bitcast.27) | data formatting | bytes 9437184
  (33 shorter events, 0.3 us)
Async XLA Ops:
  0.6 28.6 %copy-start.8 = (s32[8,128]{1,0:T(8,128)S(1)}, s32[8,128]{1,0:T(8,128)}, u32[]{:S(2)}) copy-start(s32[8,128]{1,0:T(8,128)} %refs_1_.1) | copy-start | bytes 12292
  0.6 28.6 %copy-start.12 = (f32[8,128]{1,0:T(8,128)S(1)}, f32[8,128]{1,0:T(8,128)}, u32[]{:S(2)}) copy-start(f32[8,128]{1,0:T(8,128)} %param.21) | copy-start | bytes 12292
  0.7 28.6 %copy-start.11 = (f32[8,128]{1,0:T(8,128)S(1)}, f32[8,128]{1,0:T(8,128)}, u32[]{:S(2)}) copy-start(f32[8,128]{1,0:T(8,128)} %param.20) | copy-start | bytes 12292
  4.4 25.4 %copy-start.1 = (f32[50,32,128]{2,1,0:T(8,128)S(1)}, f32[50,32,128]{2,1,0:T(8,128)}, u32[]{:S(2)}) copy-start(f32[50,32,128]{2,1,0:T(8,128)} %refs_6_.1) | copy-start | bytes 2457604
  4.4 25.4 %copy-start.2 = (f32[50,32,128]{2,1,0:T(8,128)S(1)}, f32[50,32,128]{2,1,0:T(8,128)}, u32[]{:S(2)}) copy-start(f32[50,32,128]{2,1,0:T(8,128)} %refs_7_.1) | copy-start | bytes 2457604
  4.4 25.4 %copy-start.5 = (f32[32,128]{1,0:T(8,128)S(1)}, f32[32,128]{1,0:T(8,128)}, u32[]{:S(2)}) copy-start(f32[32,128]{1,0:T(8,128)} %refs_8_.1) | copy-start | bytes 49156
  4.4 25.4 %copy-start.6 = (s32[32,128]{1,0:T(8,128)S(1)}, s32[32,128]{1,0:T(8,128)}, u32[]{:S(2)}) copy-start(s32[32,128]{1,0:T(8,128)} %refs_10_.1) | copy-start | bytes 49156
  4.4 25.4 %copy-start.9 = (f32[50]{0:T(128)S(1)}, f32[50]{0:T(128)}, u32[]{:S(2)}) copy-start(f32[50]{0:T(128)} %refs_12_.1) | copy-start | bytes 604
  4.4 25.4 %copy-start.10 = (f32[50]{0:T(128)S(1)}, f32[50]{0:T(128)}, u32[]{:S(2)}) copy-start(f32[50]{0:T(128)} %refs_14_.1) | copy-start | bytes 604
  7.6 2.3 %copy-start = (f32[36,32,8,128]{3,2,1,0:T(8,128)S(1)}, f32[36,32,8,128]{3,2,1,0:T(8,128)}, u32[]{:S(2)}) copy-start(f32[36,32,8,128]{3,2,1,0:T(8,128)} %refs_0_.1) | copy-start | bytes 14155780
  10.0 0.7 copy-start.7
  14.0 0.7 copy-start.3
  23.6 0.9 copy-start.4

commit v5 on v4

--- a/solution.py
+++ b/solution.py
@@ -256,7 +256,7 @@
     )
 
 
-CHUNKS = 4
+CHUNKS = 9
 UNROLL = 32
 LEVELS = 7
 

time: 196 us -> 192 us (0.980)
  Pallas kernels: 173 us -> 170 us
    pallas_call x1, Pallas kernels: 156 us -> 153 us  [both_steps(): pl.pallas_call(both_kernel, out_shape=(jax.ShapeDtypeStruct((bins, span_x...]
where the time goes in v5:
time: 192 us; the launch traced here: 191 us
  Pallas kernels  170 us (89%)
  local copies, waits for them, and re-layouts  18.6 us (10%)
    pallas_call x1, Pallas kernels, both_steps(): pl.pallas_call(both_kernel, out_shape=(jax.ShapeDtypeStruct((bins, span_x...  153 us
    unnamed x36, local copies, waits for them, and re-layouts  13.9 us
    pallas_call x1, Pallas kernels, remap(): pl.pallas_call(swap_kernel, out_shape=shape, in_specs=[VMEM], out_specs=V...  8.95 us
    pallas_call x1, Pallas kernels, remap(): pl.pallas_call(lambda *refs: scatter_kernel(cols, width, *refs), out_shap...  4.62 us

profile of v5, /device:TPU:18, one launch (start us, length us, event | category | flops | bytes accessed | tf_op | source)
XLA Modules:
  0.0 190.7 jit_solution(7435433780245774464)
XLA Ops:
  0.6 0.0 copy-start.8
  0.7 0.7 broadcast_divide_fusion.refs_13_
  1.4 0.1 add.53.refs_11_
  1.5 0.7 reshape.79.refs_3_.refs_1_
  2.2 0.7 reshape.80.refs_4_.refs_2_
  3.0 0.7 reshape.81.refs_5_
  3.7 0.7 slice.27
  4.4 0.0 copy-start.9
  4.4 0.8 slice.28
  5.3 0.1 copy.33
  5.4 0.1 copy.32
  5.5 0.8 copy.24
  6.3 0.8 copy.22
  7.2 0.2 copy.30
  7.4 0.2 reshape.85
  7.6 0.0 copy-start
  7.6 2.3 %copy-done = f32[36,32,8,128]{3,2,1,0:T(8,128)S(1)} copy-done((f32[36,32,8,128]{3,2,1,0:T(8,128)S(1)}, f32[36,32,8,128]{3,2,1,0:T(8,128)}, u32[]{:S(2)}) %copy-start) | copy-done | bytes 4718616
  10.0 0.7 copy-done.7
  10.6 3.4 %shard_map.156.src = f32[8,8,512]{2,1,0:T(8,128)S(1)} custom-call(f32[36,32,8,128]{3,2,1,0:T(8,128)S(1)} %copy-done, s32[8,128]{1,0:T(8,128)S(1)} %copy-done.7, f32[8,8,512]{2,1,0:T(8,128)S(1)} %concatenate.4.refs_2_, s32[8,1,512]{2,1,0:T(1,128)S(1)} %reshape.79.refs_3_.refs_1_, s32[8,1,512]{2,1,0:T(1,128)S(1)} %reshape.80.refs_4_.refs_2_, ...), custom_call_target="tpu_custom_call" | custom-call | tf_op jit(solution)/shard_map/pallas_call | solution.py:188
  14.0 0.0 copy-start.3
  14.0 0.7 copy-done.3
  14.7 9.0 %shard_map.157.refs_0_ = f32[8,8,512]{2,1,0:T(8,128)} custom-call(f32[8,8,512]{2,1,0:T(8,128)} %copy-done.3), custom_call_target="tpu_custom_call" | custom-call | tf_op jit(solution)/shard_map/pallas_call | solution.py:196
  23.6 0.9 copy-done.4
  24.5 4.6 %shard_map.158 = (f32[8,1024]{1,0:T(8,128)S(1)}, f32[8,8,512]{2,1,0:T(8,128)S(1)}) custom-call(f32[8,8,512]{2,1,0:T(8,128)S(1)} %copy-done.4, s32[8,1,512]{2,1,0:T(1,128)S(1)} %reshape.79.refs_3_.refs_1_, s32[8,1,512]{2,1,0:T(1,128)S(1)} %reshape.80.refs_4_.refs_2_), custom_call_target="tpu_custom_call" | custom-call | tf_op jit(solution)/shard_map/pallas_call | solution.py:208
  29.4 0.2 reshape.82
  29.6 0.2 copy.28
  29.7 0.1 copy.29.refs_9_
  29.9 153.4 %shard_map.159 = (f32[1152,8,128]{2,1,0:T(8,128)}, f32[50,32,128]{2,1,0:T(8,128)S(1)}, f32[50,32,128]{2,1,0:T(8,128)S(1)}, f32[32,128]{1,0:T(8,128)S(1)}) custom-call(f32[1152,8,128]{2,1,0:T(8,128)} %bitcast.26, f32[6,8,128]{2,1,0:T(8,128)S(1)} %constant_dynamic-update-slice_fusion.refs_1_, f32[36]{0:T(128)S(1)} %get-tuple-element.24.refs_2_, ...), custom_call_target="tpu_custom_call" | custom-call | tf_op jit(solution)/shard_map/pallas_call | solution.py:609
  183.3 0.9 copy.43
  184.2 0.9 copy.44
  185.1 0.6 copy.45
  185.7 5.0 %copy.46 = f32[36,32,8,128]{3,2,1,0:T(8,128)} copy(f32[36,32,8,128]{3,2,1,0:T(8,128)} %bitcast.27) | data formatting | bytes 9437184
  (33 shorter events, 0.3 us)
Async XLA Ops:
  0.6 28.6 %copy-start.8 = (s32[8,128]{1,0:T(8,128)S(1)}, s32[8,128]{1,0:T(8,128)}, u32[]{:S(2)}) copy-start(s32[8,128]{1,0:T(8,128)} %refs_1_.1) | copy-start | bytes 12292
  0.6 28.6 %copy-start.12 = (f32[8,128]{1,0:T(8,128)S(1)}, f32[8,128]{1,0:T(8,128)}, u32[]{:S(2)}) copy-start(f32[8,128]{1,0:T(8,128)} %param.21) | copy-start | bytes 12292
  0.7 28.6 %copy-start.11 = (f32[8,128]{1,0:T(8,128)S(1)}, f32[8,128]{1,0:T(8,128)}, u32[]{:S(2)}) copy-start(f32[8,128]{1,0:T(8,128)} %param.20) | copy-start | bytes 12292
  4.4 25.4 %copy-start.1 = (f32[50,32,128]{2,1,0:T(8,128)S(1)}, f32[50,32,128]{2,1,0:T(8,128)}, u32[]{:S(2)}) copy-start(f32[50,32,128]{2,1,0:T(8,128)} %refs_6_.1) | copy-start | bytes 2457604
  4.4 25.4 %copy-start.2 = (f32[50,32,128]{2,1,0:T(8,128)S(1)}, f32[50,32,128]{2,1,0:T(8,128)}, u32[]{:S(2)}) copy-start(f32[50,32,128]{2,1,0:T(8,128)} %refs_7_.1) | copy-start | bytes 2457604
  4.4 25.4 %copy-start.5 = (f32[32,128]{1,0:T(8,128)S(1)}, f32[32,128]{1,0:T(8,128)}, u32[]{:S(2)}) copy-start(f32[32,128]{1,0:T(8,128)} %refs_8_.1) | copy-start | bytes 49156
  4.4 25.4 %copy-start.6 = (s32[32,128]{1,0:T(8,128)S(1)}, s32[32,128]{1,0:T(8,128)}, u32[]{:S(2)}) copy-start(s32[32,128]{1,0:T(8,128)} %refs_10_.1) | copy-start | bytes 49156
  4.4 25.4 %copy-start.9 = (f32[50]{0:T(128)S(1)}, f32[50]{0:T(128)}, u32[]{:S(2)}) copy-start(f32[50]{0:T(128)} %refs_12_.1) | copy-start | bytes 604
  4.4 25.4 %copy-start.10 = (f32[50]{0:T(128)S(1)}, f32[50]{0:T(128)}, u32[]{:S(2)}) copy-start(f32[50]{0:T(128)} %refs_14_.1) | copy-start | bytes 604
  7.6 2.3 %copy-start = (f32[36,32,8,128]{3,2,1,0:T(8,128)S(1)}, f32[36,32,8,128]{3,2,1,0:T(8,128)}, u32[]{:S(2)}) copy-start(f32[36,32,8,128]{3,2,1,0:T(8,128)} %refs_0_.1) | copy-start | bytes 14155780
  10.0 0.7 copy-start.7
  14.0 0.7 copy-start.3
  23.6 0.9 copy-start.4
